TPU v7x, 32 devices: a whole 2x2x4 slice. The times are simulated.
32 devices in a mesh: gx: 4 (over y, core), gy: 8 (over z, x).
Axes of the slice: x: 2, y: 2, z: 4, core: 2. Of those that a mesh axis runs over, the one named last changes fastest.
Arguments:
- patches: bfloat16 [1536, 49, 512], P(('gx', 'gy')), may hold values from -6 to 6
- regions: bfloat16 [1536, 512], P(('gx', 'gy')), may hold values from -6 to 6
- send_order: int32 [32, 48], replicated, may hold values from 0 to 47, each once within a row
- image_windows: int32 [48], replicated, may hold values from 1 to 768, 1536 in all
- attn_gain: float32 [512], replicated, may hold values from 0.1 to 1.9
- attn_shift: float32 [512], replicated, may hold values from -3 to 3
- w_qkv: bfloat16 [512, 1536], replicated, may hold values from -0.25 to 0.25
- w_out: bfloat16 [512, 512], replicated, may hold values from -1 to 1
- b_out: float32 [512], replicated, may hold values from -2 to 2
- mlp_gain: float32 [512], replicated, may hold values from 0.1 to 1.9
- mlp_shift: float32 [512], replicated, may hold values from -3 to 3
- w_up: bfloat16 [512, 2048], replicated, may hold values from -0.25 to 0.25
- b_up: float32 [2048], replicated, may hold values from -3 to 3
- w_down: bfloat16 [2048, 512], replicated, may hold values from -0.125 to 0.125
- b_down: float32 [512], replicated, may hold values from -2 to 2
- upstream_patches: bfloat16 [1536, 49, 512], P(('gx', 'gy')), may hold values from -6 to 6
- upstream_regions: bfloat16 [1536, 512], P(('gx', 'gy')), may hold values from -6 to 6
Outputs:
- out_patches: bfloat16 [1536, 49, 512], P(('gx', 'gy'))
- out_regions: bfloat16 [1536, 512], P(('gx', 'gy'))
- patch_grad: bfloat16 [1536, 49, 512], P(('gx', 'gy'))
- region_grad: bfloat16 [1536, 512], P(('gx', 'gy'))
- attn_gain_grad: float32 [512], replicated
- attn_shift_grad: float32 [512], replicated
- w_qkv_grad: float32 [512, 1536], replicated
- w_out_grad: float32 [512, 512], replicated
- b_out_grad: float32 [512], replicated
- mlp_gain_grad: float32 [512], replicated
- mlp_shift_grad: float32 [512], replicated
- w_up_grad: float32 [512, 2048], replicated
- b_up_grad: float32 [2048], replicated
- w_down_grad: float32 [2048, 512], replicated
- b_down_grad: float32 [512], replicated
Inputs may be any that keep to these rules, and one draw needn't show every extreme that they name: `send_order`: each row is an ordering of its device's 48 arriving windows. `image_windows`: the sizes add up to 1536; the largest image has exactly 768 windows.
All inputs are finite; a program needn't handle non-finite values.
Results may differ from a plain program's by a relative error of at most 0.025.
Values may be sent and summed in bfloat16 or wider, within the bound.
A program may use at most 384 MiB of HBM per device.

v0:
```python
import jax
import jax.numpy as jnp
from jax import lax
from jax.sharding import PartitionSpec as P

HEADS = 16


EPS = 1e-05


def layer_norm(values, scales, offset):
    average = jnp.mean(values, axis=-1, keepdims=True)
    centered = values - average
    variance = jnp.mean(centered * centered, axis=-1, keepdims=True)
    return centered * lax.rsqrt(variance + EPS) * scales + offset


def norm_back(values, scales, offset, upstream):
    result, pullback = jax.vjp(layer_norm, values, scales, offset)
    return pullback(upstream)


def gelu_exact(values):
    return jax.nn.gelu(values, approximate=False)


def matmul(left, right):
    return jnp.dot(left, right, preferred_element_type=jnp.float32)


def contract(left, right):
    return lax.dot_general(
        left, right, (((0,), (0,)), ((), ())), preferred_element_type=jnp.float32
    )


def matmul_back(left, right):
    return lax.dot_general(
        left, right, (((1,), (1,)), ((), ())), preferred_element_type=jnp.float32
    )


def local(
    patches,
    regions,
    send_order,
    image_windows,
    attn_gain,
    attn_shift,
    w_qkv,
    w_out,
    b_out,
    mlp_gain,
    mlp_shift,
    w_up,
    b_up,
    w_down,
    b_down,
    upstream_patches,
    upstream_regions,
):
    model_width = attn_gain.shape[0]
    head_count = HEADS
    head_dim = model_width // head_count
    scaling = head_dim ** (-0.5)
    per_dev = patches.shape[0]
    seq_len = patches.shape[1] + 1
    tokens = per_dev * seq_len
    count_gx = lax.axis_size("gx")
    count_gy = lax.axis_size("gy")
    windows = per_dev * count_gx * count_gy
    per_block = per_dev // count_gx
    device_id = lax.axis_index("gx") * count_gy + lax.axis_index("gy")
    own_order = lax.dynamic_slice_in_dim(send_order, device_id, 1, 0)[0]
    target = jnp.arange(windows, dtype=jnp.int32)
    dealt_dev = target // per_dev
    within = target % per_dev
    source_dev = within // per_block * count_gy + dealt_dev % count_gy
    local_slot = send_order[source_dev, dealt_dev // count_gy * per_block + within % per_block]
    source = source_dev * per_dev + local_slot
    bounds = jnp.cumsum(image_windows)
    arrival_image = jnp.sum(
        (target[:, None] >= bounds[None, :]).astype(jnp.int32), axis=1, dtype=jnp.int32
    )
    image_all = jnp.take(arrival_image, source)
    image_own = lax.dynamic_slice_in_dim(image_all, device_id * per_dev, per_dev)
    sent_patches = jnp.take(patches, own_order, axis=0)
    sent_regions = jnp.take(regions, own_order, axis=0)
    patch_in, region_in = (
        lax.all_to_all(sent_patches, "gx", split_axis=0, concat_axis=0, tiled=True),
        lax.all_to_all(sent_regions, "gx", split_axis=0, concat_axis=0, tiled=True),
    )
    region_f = region_in.astype(jnp.float32)
    normed_r = layer_norm(region_f, attn_gain, attn_shift).astype(jnp.bfloat16)
    qkv_r = matmul(normed_r, w_qkv).astype(jnp.bfloat16)
    query_r = qkv_r[:, :model_width]
    keyval_r = qkv_r[:, model_width:]
    keyval_all = lax.all_gather(keyval_r, ("gx", "gy"), axis=0, tiled=True)
    keys_all = keyval_all[:, :model_width].reshape(windows, head_count, head_dim)
    vals_all = keyval_all[:, model_width:].reshape(windows, head_count, head_dim)
    query_heads = query_r.reshape(per_dev, head_count, head_dim)
    same_image = image_own[:, None] == image_all[None, :]
    scores_r = (
        jnp.einsum("qhe,khe->hqk", query_heads, keys_all, preferred_element_type=jnp.float32)
        * scaling
    )
    scores_r = jnp.where(same_image[None], scores_r, -1e30)
    row_top = jnp.max(scores_r, axis=-1, keepdims=True)
    weights_r = jnp.exp(scores_r - row_top)
    row_total = jnp.sum(weights_r, axis=-1, keepdims=True)
    probs_r = weights_r / row_total
    probs_low = probs_r.astype(jnp.bfloat16)
    attended_r = (
        jnp.einsum("hqk,khe->qhe", probs_low, vals_all, preferred_element_type=jnp.float32)
        .reshape(per_dev, model_width)
        .astype(jnp.bfloat16)
    )
    region_mid = region_f + matmul(attended_r, w_out) + b_out
    stacked = jnp.concatenate([region_mid[:, None, :], patch_in.astype(jnp.float32)], axis=1)
    flat_rows = stacked.reshape(tokens, model_width)
    normed_w = layer_norm(flat_rows, attn_gain, attn_shift).astype(jnp.bfloat16)
    qkv_w = (
        matmul(normed_w, w_qkv)
        .astype(jnp.bfloat16)
        .reshape(per_dev, seq_len, 3, head_count, head_dim)
    )
    local_query = qkv_w[:, :, 0]
    local_key = qkv_w[:, :, 1]
    local_value = qkv_w[:, :, 2]
    scores_w = (
        jnp.einsum("wqhe,wkhe->whqk", local_query, local_key, preferred_element_type=jnp.float32)
        * scaling
    )
    probs_w = jax.nn.softmax(scores_w, axis=-1)
    mixed_rows = (
        jnp.einsum(
            "whqk,wkhe->wqhe",
            probs_w.astype(jnp.bfloat16),
            local_value,
            preferred_element_type=jnp.float32,
        )
        .reshape(tokens, model_width)
        .astype(jnp.bfloat16)
    )
    middle = flat_rows + matmul(mixed_rows, w_out) + b_out
    normed_m = layer_norm(middle, mlp_gain, mlp_shift).astype(jnp.bfloat16)
    hidden = matmul(normed_m, w_up) + b_up
    gelu_out, gelu_pull = jax.vjp(gelu_exact, hidden)
    active = gelu_out.astype(jnp.bfloat16)
    result = middle + matmul(active, w_down) + b_down
    output = result.astype(jnp.bfloat16).reshape(per_dev, seq_len, model_width)
    upstream = jnp.concatenate([upstream_regions[:, None, :], upstream_patches], axis=1).reshape(
        tokens, model_width
    )
    grad_w_down = contract(active, upstream)
    grad_b_down = jnp.sum(upstream.astype(jnp.float32), axis=0)
    grad_active = matmul_back(upstream, w_down)
    grad_hidden = gelu_pull(grad_active)[0].astype(jnp.bfloat16)
    grad_w_up = contract(normed_m, grad_hidden)
    grad_b_up = jnp.sum(grad_hidden.astype(jnp.float32), axis=0)
    grad_normed_m = matmul_back(grad_hidden, w_up)
    grad_middle_n, grad_mlp_gain, grad_mlp_shift = norm_back(
        middle, mlp_gain, mlp_shift, grad_normed_m
    )
    grad_middle = upstream.astype(jnp.float32) + grad_middle_n
    branch_grad = grad_middle.astype(jnp.bfloat16)
    grad_w_out = contract(mixed_rows, branch_grad)
    grad_b_out = jnp.sum(branch_grad.astype(jnp.float32), axis=0)
    grad_mixed = (
        matmul_back(branch_grad, w_out)
        .astype(jnp.bfloat16)
        .reshape(per_dev, seq_len, head_count, head_dim)
    )
    grad_probs_w = jnp.einsum(
        "wqhe,wkhe->whqk", grad_mixed, local_value, preferred_element_type=jnp.float32
    )
    grad_scores_w = (
        probs_w * (grad_probs_w - jnp.sum(probs_w * grad_probs_w, axis=-1, keepdims=True))
    ).astype(jnp.bfloat16)
    grad_query = (
        jnp.einsum("whqk,wkhe->wqhe", grad_scores_w, local_key, preferred_element_type=jnp.float32)
        * scaling
    )
    grad_key = (
        jnp.einsum(
            "whqk,wqhe->wkhe", grad_scores_w, local_query, preferred_element_type=jnp.float32
        )
        * scaling
    )
    grad_value = jnp.einsum(
        "whqk,wqhe->wkhe",
        probs_w.astype(jnp.bfloat16),
        grad_mixed,
        preferred_element_type=jnp.float32,
    )
    grad_qkv_w = (
        jnp.stack([grad_query, grad_key, grad_value], axis=2)
        .astype(jnp.bfloat16)
        .reshape(tokens, 3 * model_width)
    )
    grad_w_qkv = contract(normed_w, grad_qkv_w)
    grad_normed_w = matmul_back(grad_qkv_w, w_qkv)
    grad_flat_n, gain_local, shift_local = norm_back(
        flat_rows, attn_gain, attn_shift, grad_normed_w
    )
    grad_flat = (grad_middle + grad_flat_n).reshape(per_dev, seq_len, model_width)
    patch_dealt = grad_flat[:, 1:].astype(jnp.bfloat16)
    region_mid_grad = grad_flat[:, 0]
    branch_grad_r = region_mid_grad.astype(jnp.bfloat16)
    grad_w_out = grad_w_out + contract(attended_r, branch_grad_r)
    grad_b_out = grad_b_out + jnp.sum(branch_grad_r.astype(jnp.float32), axis=0)
    grad_attended = matmul_back(branch_grad_r, w_out).astype(jnp.bfloat16)
    grad_att_heads = grad_attended.reshape(per_dev, head_count, head_dim)
    grad_probs_r = jnp.einsum(
        "qhe,khe->hqk", grad_att_heads, vals_all, preferred_element_type=jnp.float32
    )
    delta_r = jnp.sum(probs_r * grad_probs_r, axis=-1, keepdims=True)
    grad_scores_r = (probs_r * (grad_probs_r - delta_r)).astype(jnp.bfloat16)
    grad_query_r = (
        jnp.einsum(
            "hqk,khe->qhe", grad_scores_r, keys_all, preferred_element_type=jnp.float32
        ).reshape(per_dev, model_width)
        * scaling
    )
    grad_keys = (
        jnp.einsum("hqk,qhe->khe", grad_scores_r, query_heads, preferred_element_type=jnp.float32)
        * scaling
    )
    grad_vals = jnp.einsum(
        "hqk,qhe->khe", probs_low, grad_att_heads, preferred_element_type=jnp.float32
    )
    grad_keyval = lax.psum_scatter(
        jnp.concatenate(
            [
                grad_keys.reshape(per_dev * lax.axis_size(("gx", "gy")), model_width),
                grad_vals.reshape(per_dev * lax.axis_size(("gx", "gy")), model_width),
            ],
            axis=1,
        ),
        ("gx", "gy"),
        scatter_dimension=0,
        tiled=True,
    )
    grad_qkv_r = jnp.concatenate([grad_query_r, grad_keyval], axis=1).astype(jnp.bfloat16)
    grad_w_qkv = grad_w_qkv + contract(normed_r, grad_qkv_r)
    grad_normed_r = matmul_back(grad_qkv_r, w_qkv)
    grad_region_n, gain_region, shift_region = norm_back(
        region_f, attn_gain, attn_shift, grad_normed_r
    )
    region_dealt = (region_mid_grad + grad_region_n).astype(jnp.bfloat16)
    grad_attn_gain = gain_local + gain_region
    grad_attn_shift = shift_local + shift_region
    (
        grad_attn_gain,
        grad_attn_shift,
        grad_w_qkv,
        grad_w_out,
        grad_b_out,
        grad_mlp_gain,
        grad_mlp_shift,
        grad_w_up,
        grad_b_up,
        grad_w_down,
        grad_b_down,
    ) = lax.psum(
        (
            grad_attn_gain,
            grad_attn_shift,
            grad_w_qkv,
            grad_w_out,
            grad_b_out,
            grad_mlp_gain,
            grad_mlp_shift,
            grad_w_up,
            grad_b_up,
            grad_w_down,
            grad_b_down,
        ),
        ("gx", "gy"),
    )
    back_patches, back_regions = (
        lax.all_to_all(patch_dealt, "gx", split_axis=0, concat_axis=0, tiled=True),
        lax.all_to_all(region_dealt, "gx", split_axis=0, concat_axis=0, tiled=True),
    )
    chooser = (own_order[:, None] == jnp.arange(per_dev, dtype=jnp.int32)[None, :]).astype(
        jnp.bfloat16
    )
    patch_grad = (
        contract(chooser, back_patches.reshape(per_dev, -1))
        .astype(jnp.bfloat16)
        .reshape(patches.shape)
    )
    region_grad = contract(chooser, back_regions).astype(jnp.bfloat16)
    return (
        output[:, 1:],
        output[:, 0],
        patch_grad,
        region_grad,
        grad_attn_gain,
        grad_attn_shift,
        grad_w_qkv,
        grad_w_out,
        grad_b_out,
        grad_mlp_gain,
        grad_mlp_shift,
        grad_w_up,
        grad_b_up,
        grad_w_down,
        grad_b_down,
    )


def solution(mesh):
    in_specs = (
        P(("gx", "gy"), None, None),
        P(("gx", "gy"), None),
        P(),
        P(),
        P(),
        P(),
        P(),
        P(),
        P(),
        P(),
        P(),
        P(),
        P(),
        P(),
        P(),
        P(("gx", "gy"), None, None),
        P(("gx", "gy"), None),
    )
    out_specs = (
        P(("gx", "gy"), None, None),
        P(("gx", "gy"), None),
        P(("gx", "gy"), None, None),
        P(("gx", "gy"), None),
        P(),
        P(),
        P(),
        P(),
        P(),
        P(),
        P(),
        P(),
        P(),
        P(),
        P(),
    )
    return jax.shard_map(local, mesh=mesh, in_specs=in_specs, out_specs=out_specs, check_vma=False)
```

profile of v0, /device:TPU:0, one launch (start us, length us, event | category | flops | bytes accessed | tf_op | source)
XLA Modules:
  0.0 968.8 jit_solution(6543252691517621669)
XLA Ops:
  11.0 8.2 all_to_all.28
  22.8 11.2 %gather_fusion.3 = bf16[48,49,512]{2,0,1:T(8,128)(2,1)} fusion(bf16[48,49,512]{2,0,1:T(8,128)(2,1)S(1)} %copy-done, s32[1024]{0:T(1024)S(1)} %pad_clamp_fusion.1), kind=kCustom, calls=%fused_computation.3 | custom fusion | bytes 4817088 | tf_op jit(solution)/shard_map/jit(_take)/gather | solution.py:88
  38.9 4.8 all-to-all-start.1
  43.9 10.3 %gather_fusion.1 = s32[1536]{0:T(1024)S(1)} fusion(s32[32,48]{1,0:T(8,128)S(1)} %copy-done.2, s32[1536]{0:T(1024)S(1)} %fusion.92), kind=kCustom, calls=%fused_computation.1 | custom fusion | bytes 24576 | tf_op jit(solution)/shard_map/gather | solution.py:80
  59.4 4.2 reshape.677
  63.8 8.4 gather_fusion.2
  72.6 10.8 %all-to-all-done.1 = bf16[48,49,512]{2,1,0:T(8,128)(2,1)} async-done(((bf16[48,49,512]{2,1,0:T(8,128)(2,1)}), bf16[48,49,512]{2,1,0:T(8,128)(2,1)}, u32[]{:S(2)}, u32[]{:S(2)}) %all-to-all-start.1) | async-done | bytes 2408480 | tf_op jit(solution)/shard_map/all_to_all | solution.py:91
  83.4 5.0 convert_element_type.153
  88.4 3.7 fusion.110
  93.9 3.1 copy.179
  97.0 3.8 fusion.111
  100.9 3.7 fusion.52
  105.0 5.6 fusion.107
  110.7 3.4 multiply_reduce_fusion.2
  114.1 5.7 reshape.674
  120.7 9.5 convolution_convert_fusion.1
  130.2 32.3 %reshape.718 = bf16[48,50,3,16,32]{4,3,2,1,0:T(8,128)(2,1)} reshape(bf16[2400,1536]{1,0:T(8,128)(2,1)} %convolution_convert_fusion.1) | data formatting | bytes 14745600 | tf_op jit(solution)/shard_map/reshape | solution.py:126
  162.5 22.4 %fusion.109 = (bf16[48,50,1,16,32]{4,3,2,1,0:T(8,128)(2,1)}, bf16[48,50,1,16,32]{4,3,2,1,0:T(8,128)(2,1)}, bf16[48,50,1,16,32]{4,3,2,1,0:T(8,128)(2,1)}) fusion(bf16[48,50,3,16,32]{4,3,2,1,0:T(8,128)(2,1)} %reshape.718), kind=kLoop, calls=%fused_computation.217 | loop fusion | bytes 14745600 | tf_op jit(solution)/shard_map/slice | solution.py:128
  184.9 13.9 %copy.227 = bf16[48,50,1,16,32]{1,4,3,0,2:T(8,128)(2,1)} copy(bf16[48,50,1,16,32]{4,3,2,1,0:T(8,128)(2,1)} %get-tuple-element.139) | data formatting | bytes 4915200
  198.8 13.9 %copy.226 = bf16[48,50,1,16,32]{1,4,3,0,2:T(8,128)(2,1)} copy(bf16[48,50,1,16,32]{4,3,2,1,0:T(8,128)(2,1)} %get-tuple-element.140) | data formatting | bytes 4915200
  212.7 13.9 %copy.228 = bf16[48,50,1,16,32]{1,4,3,0,2:T(8,128)(2,1)} copy(bf16[48,50,1,16,32]{4,3,2,1,0:T(8,128)(2,1)} %get-tuple-element.141) | data formatting | bytes 4915200
  226.7 13.3 %fusion.14 = f32[48,16,50,50]{2,3,1,0:T(8,128)} fusion(bf16[48,50,1,16,32]{1,4,3,0,2:T(8,128)(2,1)} %copy.228, bf16[48,50,1,16,32]{1,4,3,0,2:T(8,128)(2,1)} %copy.227), kind=kOutput, calls=%fused_computation.41 | convolution fusion | flops 122880000 | bytes 12595200 | tf_op jit(solution)/shard_map/wqhe,wkhe->whqk/dot_general | solution.py:132
  240.0 27.4 %fusion.112 = (f32[48,16,50]{2,1,0:T(8,128)S(1)}, f32[48,16,50,50]{2,3,1,0:T(8,128)}) fusion(f32[48,16,50,50]{2,3,1,0:T(8,128)} %fusion.14), kind=kOutput, calls=%fused_computation.220 | output fusion | flops 7680049 | bytes 15513600 | tf_op jit(solution)/shard_map/sub | solution.py:135
  267.4 13.8 %convert_bitcast_fusion = bf16[48,50,16,32]{1,3,2,0:T(8,128)(2,1)} fusion(bf16[48,50,1,16,32]{1,4,3,0,2:T(8,128)(2,1)} %copy.226, f32[48,16,50,50]{2,3,1,0:T(8,128)} %get-tuple-element.151, f32[48,16,50]{2,1,0:T(8,128)S(1)} %get-tuple-element.150), kind=kOutput, calls=%fused_computation.50 | convolution fusion | flops 127948800 | bytes 12748800 | tf_op jit(solution)/shard_map/whqk,wkhe->wqhe/dot_general | solution.py:137
  281.2 9.5 copy.194
  290.7 9.2 convert_element_type.159
  299.9 4.9 fusion.113
  307.9 50.8 %multiply_convert_fusion.1 = (bf16[2400,2048]{1,0:T(8,128)(2,1)}, f32[2400,2048]{1,0:T(8,128)}, f32[2400,2048]{1,0:T(8,128)}) fusion(f32[2048]{0:T(1024)S(1)} %copy-done.72, bf16[512,2048]{1,0:T(8,128)(2,1)S(1)} %copy-done.70, f32[2400,512]{1,0:T(8,128)S(1)} %get-tuple-element.153, f32[512]{0:T(512)S(1)} %copy-done.73, f32[512]{0:T(512)S(1)} %copy-done.63, ...), kind=kOutput, calls=%fused_computation.15 | convolution fusion | flops 5363712000 | bytes 56195840 | tf_op jit(solution)/shard_map/dot_general | solution.py:29
  358.7 22.7 %convert_reduce_fusion = (f32[2048]{0:T(1024)}, bf16[2400,2048]{1,0:T(8,128)(2,1)}) fusion(f32[2400,2048]{1,0:T(8,128)} %get-tuple-element.134, bf16[2400,512]{1,0:T(8,128)(2,1)S(1)} %copy-done.5, bf16[2048,512]{1,0:T(8,128)(2,1)} %param.30, f32[2400,2048]{1,0:T(8,128)} %get-tuple-element.154, f32[2048]{0:T(1024)S(1)} %copy-done.72), kind=kOutput, calls=%fused_computation.13 | convolution fusion | flops 5116721152 | bytes 53723136 | tf_op jit(solution)/shard_map/dot_general | solution.py:39
  381.5 12.2 %multiply_reduce_fusion.3 = (f32[512]{0:T(512)}, f32[2400]{0:T(1024)S(1)}, f32[512]{0:T(512)}, f32[2400,512]{1,0:T(8,128)S(1)}) fusion(f32[2400,512]{1,0:T(8,128)S(1)} %get-tuple-element.153, f32[2400]{0:T(1024)S(1)} %fusion.69, f32[2400]{0:T(1024)S(1)} %broadcast_multiply_fusion.1, f32[512]{0:T(512)S(1)} %copy-done.63, ...), kind=kOutput, calls=%fused_computation.60 | convolution fusion | flops 5042991616 | bytes 21792896 | tf_op jit(solution)/shard_map/dot_general | solution.py:39
  402.5 11.8 %reshape.719 = bf16[48,50,16,32]{3,2,1,0:T(8,128)(2,1)} reshape(bf16[2400,512]{1,0:T(8,128)(2,1)} %convolution_convert_fusion.2) | data formatting | bytes 4915200 | tf_op jit(solution)/shard_map/reshape | solution.py:173
  414.3 14.0 %copy.197 = bf16[48,50,16,32]{1,3,2,0:T(8,128)(2,1)} copy(bf16[48,50,16,32]{3,2,1,0:T(8,128)(2,1)} %reshape.719) | data formatting | bytes 4915200 | tf_op jit(solution)/shard_map/reshape | solution.py:173
  428.3 13.9 %fusion.27 = bf16[48,50,1,16,32]{1,4,3,0,2:T(8,128)(2,1)} fusion(bf16[48,50,16,32]{1,3,2,0:T(8,128)(2,1)} %copy.197, f32[48,16,50,50]{2,3,1,0:T(8,128)} %get-tuple-element.151, f32[48,16,50]{2,1,0:T(8,128)S(1)} %copy-done.22), kind=kOutput, calls=%fused_computation.77 | convolution fusion | flops 126720000 | bytes 12748800 | tf_op jit(solution)/shard_map/whqk,wqhe->wkhe/dot_general | solution.py:191
  442.1 21.6 %multiply_reduce_fusion = (f32[48,16,50]{2,1,0:T(8,128)S(1)}, f32[48,16,50,50]{2,3,1,0:T(8,128)}) fusion(f32[48,16,50,50]{2,3,1,0:T(8,128)} %get-tuple-element.151, f32[48,16,50]{2,1,0:T(8,128)S(1)} %copy-done.22, bf16[48,50,16,32]{1,3,2,0:T(8,128)(2,1)} %copy.197, bf16[48,50,1,16,32]{1,4,3,0,2:T(8,128)(2,1)} %copy.226), kind=kOutput, calls=%fused_computation.10 | convolution fusion | flops 128601600 | bytes 20582400 | tf_op jit(solution)/shard_map/wqhe,wkhe->whqk/dot_general | solution.py:175
  463.8 18.6 %multiply_convert_fusion = bf16[48,16,50,50]{2,3,1,0:T(8,128)(2,1)} fusion(f32[48,16,50,50]{2,3,1,0:T(8,128)} %get-tuple-element.157, f32[48,16,50]{2,1,0:T(8,128)S(1)} %get-tuple-element.156, f32[48,16,50,50]{2,3,1,0:T(8,128)} %get-tuple-element.151, f32[48,16,50]{2,1,0:T(8,128)S(1)} %copy-done.22), kind=kLoop, calls=%fused_computation.9 | loop fusion | flops 7680000 | bytes 19507200 | tf_op jit(solution)/shard_map/convert_element_type | solution.py:180
  482.4 9.9 %multiply_bitcast_fusion = bf16[48,50,1,16,32]{1,4,3,0,2:T(8,128)(2,1)S(1)} fusion(bf16[48,16,50,50]{2,3,1,0:T(8,128)(2,1)} %multiply_convert_fusion, bf16[48,50,1,16,32]{1,4,3,0,2:T(8,128)(2,1)} %copy.227), kind=kOutput, calls=%fused_computation.31 | convolution fusion | flops 125337600 | bytes 8755200 | tf_op jit(solution)/shard_map/whqk,wqhe->wkhe/dot_general | solution.py:186
  492.3 11.7 %multiply_bitcast_fusion.1 = bf16[48,50,1,16,32]{1,4,3,0,2:T(8,128)(2,1)} fusion(bf16[48,16,50,50]{2,3,1,0:T(8,128)(2,1)} %multiply_convert_fusion, bf16[48,50,1,16,32]{1,4,3,0,2:T(8,128)(2,1)} %copy.228), kind=kOutput, calls=%fused_computation.32 | convolution fusion | flops 125337600 | bytes 8755200 | tf_op jit(solution)/shard_map/whqk,wkhe->wqhe/dot_general | solution.py:182
  504.0 8.8 maximum_convert_fusion
  512.8 12.8 %copy.202 = bf16[48,50,3,16,32]{1,0,4,3,2:T(8,128)(2,1)} copy(bf16[48,50,3,16,32]{1,4,3,0,2:T(8,128)(2,1)S(1)} %maximum_convert_fusion) | data formatting | bytes 14745600 | tf_op jit(solution)/shard_map/convert_element_type | solution.py:199
  525.6 25.4 %convert_element_type.169 = bf16[2400,1536]{0,1:T(8,128)(2,1)} reshape(bf16[48,50,3,16,32]{1,0,4,3,2:T(8,128)(2,1)} %copy.202) | data formatting | bytes 14745600 | tf_op jit(solution)/shard_map/convert_element_type | solution.py:199
  551.1 11.2 %multiply_reduce_fusion.4 = (f32[512]{0:T(512)S(1)}, f32[2400]{0:T(1024)S(1)}, f32[512]{0:T(512)S(1)}, f32[2400,512]{1,0:T(8,128)S(1)}) fusion(f32[2400,512]{1,0:T(8,128)} %reshape.674, f32[2400]{0:T(1024)S(1)} %copy-done.47, f32[2400]{0:T(1024)S(1)} %copy-done.49, f32[512]{0:T(512)S(1)} %copy-done.43, bf16[2400,1536]{0,1:T(8,128)(2,1)} %convert_element_type.169, ...), kind=kOutput, calls=%fused_computation.62 | convolution fusion | flops 3784700672 | bytes 18811008 | tf_op jit(solution)/shard_map/dot_general | solution.py:39
  564.5 4.8 add_add_fusion.2
  569.2 5.5 reshape.679
  576.3 3.1 fusion.47
  582.8 3.0 pad_maximum_fusion
  585.8 6.6 copy.215
  593.1 4.4 add_convert_fusion.1
  597.5 4.4 convert_element_type.177
  604.3 4.3 fusion.115
  609.9 9.5 fusion.114
  619.4 7.5 fusion.100
  626.9 10.0 %fusion.116 = f32[2048,512]{1,0:T(8,128)} fusion(bf16[2400,2048]{1,0:T(8,128)(2,1)} %get-tuple-element.133, bf16[2400,512]{1,0:T(8,128)(2,1)S(1)} %copy-done.7), kind=kOutput, calls=%fused_computation.224 | convolution fusion | flops 5033164800 | bytes 16482304 | tf_op jit(solution)/shard_map/dot_general | solution.py:33
  637.0 70.3 %reduce-scatter.4.cloned.1.call-done = f32[48,1024]{1,0:T(8,128)} async-done(((f32[1536,1024]{1,0:T(8,128)}), f32[48,1024]{1,0:T(8,128)}) %reduce-scatter.4.cloned.1.call-update) | async-done | bytes 196624 | tf_op jit(solution)/shard_map/reduce_scatter | solution.py:233
  708.3 4.2 convolution_add_fusion.1
  714.6 5.3 slice.65
  719.9 4.6 all-to-all-start.2
  724.5 11.6 %add_convert_fusion.2 = bf16[2400,512]{1,0:T(8,128)(2,1)} fusion(f32[2400,512]{1,0:T(8,128)} %copy-done.3, bf16[2400,2048]{1,0:T(8,128)(2,1)} %get-tuple-element.133, bf16[2048,512]{1,0:T(8,128)(2,1)S(1)} %copy-done.71, f32[512]{0:T(512)S(1)} %copy-done.75), kind=kOutput, calls=%fused_computation.67 | convolution fusion | flops 5036851200 | bytes 19302400 | tf_op jit(solution)/shard_map/dot_general | solution.py:29
  736.1 4.3 reshape.676
  741.4 3.4 slice.60
  747.7 29.5 %all-to-all-done.2 = bf16[48,49,512]{2,1,0:T(8,128)(2,1)} async-done(((bf16[48,49,512]{2,1,0:T(8,128)(2,1)}), bf16[48,49,512]{2,1,0:T(8,128)(2,1)}, u32[]{:S(2)}, u32[]{:S(2)}) %all-to-all-start.2) | async-done | bytes 2408480 | tf_op jit(solution)/shard_map/all_to_all | solution.py:283
  783.0 3.4 all-to-all-start.3
  789.1 43.3 %all-reduce = (f32[512]{0:T(512)}, f32[512]{0:T(512)}, f32[512]{0:T(512)}, f32[512]{0:T(512)}, f32[512]{0:T(512)}, /*index=5*/f32[2048]{0:T(1024)}, f32[512]{0:T(512)}) all-reduce(f32[512]{0:T(512)S(1)} %add.471, f32[512]{0:T(512)S(1)} %add.472, f32[512]{0:T(512)S(1)} %add.477, ...), channel_id=1, replica_groups=mesh['gx'=4,'gy'=8] {'gx','gy'}, use_global_device_ids=true, to_apply=%region_23.24 | all-reduce | flops 5120 | bytes 40960 | tf_op jit(solution)/shard_map/psum | solution.py:266
  833.3 118.5 %all-reduce.4.cloned.1.call-done = (f32[512,1536]{1,0:T(8,128)}, f32[512,512]{1,0:T(8,128)}, f32[512,2048]{1,0:T(8,128)}, f32[2048,512]{1,0:T(8,128)}) async-done(((f32[512,1536]{1,0:T(8,128)}, f32[512,512]{1,0:T(8,128)}, f32[512,2048]{1,0:T(8,128)}, f32[2048,512]{1,0:T(8,128)}), (f32[512,1536]{1,0:T(8,128)}, f32[512,512]{1,0:T(8,128)}, f32[512,2048]{1,0:T(8,128)}, ...) | async-done | bytes 12582928 | tf_op jit(solution)/shard_map/psum | solution.py:266
  951.9 3.9 copy.249
  (268 shorter events, 66.7 us)
Async XLA Ops:
  7.2 15.6 %copy-start = (bf16[48,49,512]{2,0,1:T(8,128)(2,1)S(1)}, bf16[48,49,512]{2,0,1:T(8,128)(2,1)}, u32[]{:S(2)}) copy-start(bf16[48,49,512]{2,0,1:T(8,128)(2,1)} %param.17) | copy-start | bytes 7225348
  7.2 81.2 %all-gather.2.cloned.1.call-start = ((), (), s32[]{:S(2)}) async-start(), calls=%async_computation.5 | async-start | bytes 3244032 | tf_op jit(solution)/shard_map/all_gather | solution.py:99
  9.3 24.7 %copy-start.61 = (s32[1,48]{1,0:T(1,128)}, s32[1,48]{1,0:T(1,128)S(1)}, u32[]{:S(2)}) copy-start(s32[1,48]{1,0:T(1,128)S(1)} %get-tuple-element.138) | copy-start | bytes 580
  19.3 14.6 %copy-start.53 = (f32[48]{0:T(128)}, f32[48]{0:T(128)S(1)}, u32[]{:S(2)}) copy-start(f32[48]{0:T(128)S(1)} %div.149) | copy-start | bytes 580
  20.1 13.8 %copy-start.55 = (f32[48]{0:T(128)}, f32[48]{0:T(128)S(1)}, u32[]{:S(2)}) copy-start(f32[48]{0:T(128)S(1)} %rsqrt.36) | copy-start | bytes 580
  20.1 84.4 %copy-start.17 = (f32[48,512]{1,0:T(8,128)}, f32[48,512]{1,0:T(8,128)S(1)}, u32[]{:S(2)}) copy-start(f32[48,512]{1,0:T(8,128)S(1)} %reshape.685) | copy-start | bytes 294916
  35.9 8.0 copy-start.2
  38.9 44.6 %all-to-all-start.1 = ((bf16[48,49,512]{2,1,0:T(8,128)(2,1)}), bf16[48,49,512]{2,1,0:T(8,128)(2,1)}, u32[]{:S(2)}, u32[]{:S(2)}) async-start(bf16[48,49,512]{2,1,0:T(8,128)(2,1)} %copy.183), calls=%async_computation.1 | async-start | bytes 5505024 | tf_op jit(solution)/shard_map/all_to_all | solution.py:91
  43.7 10.6 %copy-start.67 = (s32[48]{0:T(128)S(1)}, s32[48]{0:T(128)}, u32[]{:S(2)}) copy-start(s32[48]{0:T(128)} %param.20) | copy-start | bytes 580
  43.7 10.9 %copy-start.31 = (bf16[48,512]{1,0:T(8,128)(2,1)S(1)}, bf16[48,512]{1,0:T(8,128)(2,1)}, u32[]{:S(2)}) copy-start(bf16[48,512]{1,0:T(8,128)(2,1)} %param.33) | copy-start | bytes 147460
  43.7 663.6 %reduce-scatter.4.cloned.1.call-start = ((), (), s32[]{:S(2)}) async-start(), calls=%async_computation.6 | async-start | bytes 6488064 | tf_op jit(solution)/shard_map/reduce_scatter | solution.py:233
  72.6 24.4 %copy-start.25 = (bf16[48,512]{0,1:T(8,128)(2,1)}, bf16[48,512]{0,1:T(8,128)(2,1)S(1)}, u32[]{:S(2)}) copy-start(bf16[48,512]{0,1:T(8,128)(2,1)S(1)} %copy.217) | copy-start | bytes 147460
  93.9 7.0 copy-start.11
  104.6 6.0 copy-start.27
  110.6 9.3 copy-start.29
  110.7 10.0 %copy-start.48 = (f32[2400]{0:T(1024)}, f32[2400]{0:T(1024)S(1)}, u32[]{:S(2)}) copy-start(f32[2400]{0:T(1024)S(1)} %div.162) | copy-start | bytes 28804
  114.1 6.5 copy-start.9
  114.1 6.5 copy-start.42
  114.1 6.5 copy-start.51
  120.6 9.6 copy-start.39
  120.7 9.5 copy-start.46
  267.4 13.8 %copy-start.21 = (f32[48,16,50]{2,1,0:T(8,128)}, f32[48,16,50]{2,1,0:T(8,128)S(1)}, u32[]{:S(2)}) copy-start(f32[48,16,50]{2,1,0:T(8,128)S(1)} %get-tuple-element.150) | copy-start | bytes 460804
  304.7 88.9 %copy-start.3 = (f32[2400,512]{1,0:T(8,128)}, f32[2400,512]{1,0:T(8,128)S(1)}, u32[]{:S(2)}) copy-start(f32[2400,512]{1,0:T(8,128)S(1)} %get-tuple-element.153) | copy-start | bytes 14745604
  304.8 88.9 %copy-start.33 = (f32[2400]{0:T(1024)}, f32[2400]{0:T(1024)S(1)}, u32[]{:S(2)}) copy-start(f32[2400]{0:T(1024)S(1)} %broadcast_multiply_fusion.1) | copy-start | bytes 28804
  305.8 52.9 %copy-start.37 = (f32[2400]{0:T(1024)}, f32[2400]{0:T(1024)S(1)}, u32[]{:S(2)}) copy-start(f32[2400]{0:T(1024)S(1)} %multiply_reduce_fusion.7) | copy-start | bytes 28804
  307.9 85.7 %copy-start.44 = (f32[2400]{0:T(1024)}, f32[2400]{0:T(1024)S(1)}, u32[]{:S(2)}) copy-start(f32[2400]{0:T(1024)S(1)} %fusion.69) | copy-start | bytes 28804
  307.9 50.8 %copy-start.5 = (bf16[2400,512]{1,0:T(8,128)(2,1)S(1)}, bf16[2400,512]{1,0:T(8,128)(2,1)}, u32[]{:S(2)}) copy-start(bf16[2400,512]{1,0:T(8,128)(2,1)} %reshape.677) | copy-start | bytes 7372804
  381.5 12.2 %copy-start.38 = (f32[2400]{0:T(1024)S(1)}, f32[2400]{0:T(1024)}, u32[]{:S(2)}) copy-start(f32[2400]{0:T(1024)} %copy-done.37) | copy-start | bytes 28804
  414.3 14.0 %copy-start.22 = (f32[48,16,50]{2,1,0:T(8,128)S(1)}, f32[48,16,50]{2,1,0:T(8,128)}, u32[]{:S(2)}) copy-start(f32[48,16,50]{2,1,0:T(8,128)} %copy-done.21) | copy-start | bytes 460804
  525.6 25.4 %copy-start.10 = (bf16[512,1536]{1,0:T(8,128)(2,1)S(1)}, bf16[512,1536]{1,0:T(8,128)(2,1)}, u32[]{:S(2)}) copy-start(bf16[512,1536]{1,0:T(8,128)(2,1)} %param.23) | copy-start | bytes 4718596
  525.6 25.4 %copy-start.43 = (f32[512]{0:T(512)S(1)}, f32[512]{0:T(512)}, u32[]{:S(2)}) copy-start(f32[512]{0:T(512)} %param.21) | copy-start | bytes 6148
  525.6 25.5 %copy-start.47 = (f32[2400]{0:T(1024)S(1)}, f32[2400]{0:T(1024)}, u32[]{:S(2)}) copy-start(f32[2400]{0:T(1024)} %copy-done.46) | copy-start | bytes 28804
  525.6 25.5 %copy-start.49 = (f32[2400]{0:T(1024)S(1)}, f32[2400]{0:T(1024)}, u32[]{:S(2)}) copy-start(f32[2400]{0:T(1024)} %copy-done.48) | copy-start | bytes 28804
  525.6 36.7 %slice-start = ((s8[4915200]{0:T(1024)(128)(4,1)}), s8[720896]{0:T(1024)(128)(4,1)S(1)}, s32[]{:S(2)}) async-start(s8[4915200]{0:T(1024)(128)(4,1)} %bitcast.136), calls=%async_computation.8 | async-start | bytes 1441792
  551.0 11.2 %copy-start.40 = (f32[2400]{0:T(1024)S(1)}, f32[2400]{0:T(1024)}, u32[]{:S(2)}) copy-start(f32[2400]{0:T(1024)} %copy-done.39) | copy-start | bytes 28804
  551.0 11.2 %slice-start.1 = ((s8[4915200]{0:T(1024)(128)(4,1)}), s8[4194304]{0:T(1024)(128)(4,1)S(1)}, s32[]{:S(2)}) async-start(s8[4915200]{0:T(1024)(128)(4,1)} %bitcast.136), calls=%async_computation.9 | async-start | bytes 8388608
  569.2 6.7 copy-start.14
  569.2 7.1 copy-start.60
  569.2 10.2 %slice-start.4 = ((s8[4718592]{0:T(1024)(128)(4,1)}), s8[524288]{0:T(1024)(128)(4,1)S(1)}, s32[]{:S(2)}) async-start(s8[4718592]{0:T(1024)(128)(4,1)} %bitcast.145), calls=%async_computation.12 | async-start | bytes 1048576
  592.4 359.5 %all-reduce.4.cloned.1.call-start = ((), (), s32[]{:S(2)}) async-start(), calls=%async_computation.7 | async-start | bytes 25165824 | tf_op jit(solution)/shard_map/psum | solution.py:266
  604.2 5.6 copy-start.19
  604.3 15.1 %slice-start.2 = ((s8[4915200]{0:T(1024)(128)(4,1)}), s8[4194304]{0:T(1024)(128)(4,1)S(1)}, s32[]{:S(2)}) async-start(s8[4915200]{0:T(1024)(128)(4,1)} %bitcast.138), calls=%async_computation.10 | async-start | bytes 8388608
  604.3 15.1 %slice-start.6 = ((s8[9830400]{0:T(1024)(128)(4,1)}), s8[4194304]{0:T(1024)(128)(4,1)S(1)}, s32[]{:S(2)}) async-start(s8[9830400]{0:T(1024)(128)(4,1)} %bitcast.164), calls=%async_computation.14 | async-start | bytes 8388608
  609.8 9.5 slice-start.3
  609.8 9.5 copy-start.34
  609.8 9.5 copy-start.45
  609.8 9.5 copy-start.64
  609.8 9.5 copy-start.74
  609.8 9.5 slice-start.7
  609.9 9.5 slice-start.8
  619.4 7.5 copy-start.7
  626.9 81.3 %copy-start.18 = (f32[48,512]{1,0:T(8,128)S(1)}, f32[48,512]{1,0:T(8,128)}, u32[]{:S(2)}) copy-start(f32[48,512]{1,0:T(8,128)} %copy-done.17) | copy-start | bytes 294916
  626.9 81.3 %copy-start.54 = (f32[48]{0:T(128)S(1)}, f32[48]{0:T(128)}, u32[]{:S(2)}) copy-start(f32[48]{0:T(128)} %copy-done.53) | copy-start | bytes 580
  626.9 81.3 %copy-start.56 = (f32[48]{0:T(128)S(1)}, f32[48]{0:T(128)}, u32[]{:S(2)}) copy-start(f32[48]{0:T(128)} %copy-done.55) | copy-start | bytes 580
  714.6 9.9 %copy-start.71 = (bf16[2048,512]{1,0:T(8,128)(2,1)S(1)}, bf16[2048,512]{1,0:T(8,128)(2,1)}, u32[]{:S(2)}) copy-start(bf16[2048,512]{1,0:T(8,128)(2,1)} %param.30) | copy-start | bytes 6291460
  714.6 9.9 %copy-start.75 = (f32[512]{0:T(512)S(1)}, f32[512]{0:T(512)}, u32[]{:S(2)}) copy-start(f32[512]{0:T(512)} %param.31) | copy-start | bytes 6148
  719.9 57.3 %all-to-all-start.2 = ((bf16[48,49,512]{2,1,0:T(8,128)(2,1)}), bf16[48,49,512]{2,1,0:T(8,128)(2,1)}, u32[]{:S(2)}, u32[]{:S(2)}) async-start(bf16[48,49,512]{2,1,0:T(8,128)(2,1)} %slice.65), calls=%async_computation.2 | async-start | bytes 5505024 | tf_op jit(solution)/shard_map/all_to_all | solution.py:283
  745.4 36.6 %copy-start.69 = (f32[48]{0:T(128)S(1)}, f32[48]{0:T(128)}, u32[]{:S(2)}) copy-start(f32[48]{0:T(128)} %copy-done.68) | copy-start | bytes 580
  747.7 38.7 %copy-start.62 = (s32[1,48]{1,0:T(1,128)S(1)}, s32[1,48]{1,0:T(1,128)}, u32[]{:S(2)}) copy-start(s32[1,48]{1,0:T(1,128)} %copy-done.61) | copy-start | bytes 580
  783.0 6.1 copy-start.57
  783.0 6.1 copy-start.58
  783.0 6.1 copy-start.65
  783.0 6.1 copy-start.66
  783.0 49.5 %all-to-all-start.3 = ((bf16[4,12,512]{2,1,0:T(8,128)(2,1)}), bf16[4,12,512]{2,1,0:T(8,128)(2,1)S(1)}, u32[]{:S(2)}, u32[]{:S(2)}) async-start(bf16[4,12,512]{2,1,0:T(8,128)(2,1)} %all_to_all.21), calls=%async_computation.3 | async-start | bytes 131072 | tf_op jit(solution)/shard_map/all_to_all | solution.py:284
  (27 other events, 72.8 us)
Sparse Core Ops, SparseCore 0:
  22.9 64.6 all-gather.1
  592.5 114.7 reduce-scatter.3
  716.0 235.8 all-reduce.3
where the time goes:
time: 983 us; the launch traced here: 969 us
  local copies, waits for them, and re-layouts  296 us (30%)
  matrix products  267 us (27%)
  waiting for transfers between devices  229 us (23%)
  other arithmetic  96.4 us (10%)
  blocking collectives  51.5 us (5%)
  between operations  15.4 us (2%)
  starting transfers between devices  12.9 us (1%)
    psum x1, waiting for transfers between devices, local(): lax.psum((grad_attn_gain, grad_attn_shift, grad_w_qkv, grad_w_out, grad_b...  119 us
    dot_general x6, matrix products, matmul(): return jnp.dot(left, right, preferred_element_type=jnp.float32)  78.9 us
    unnamed x181, local copies, waits for them, and re-layouts  71.8 us
    reduce_scatter x1, waiting for transfers between devices, local(): lax.psum_scatter(jnp.concatenate([grad_keys.reshape(per_dev * lax.axis_si...  70.3 us
    dot_general x6, matrix products, matmul_back(): lax.dot_general(left, right, (((1,), (1,)), ((), ())), preferred_element_...  51.4 us
    psum x1, blocking collectives, local(): lax.psum((grad_attn_gain, grad_attn_shift, grad_w_qkv, grad_w_out, grad_b...  43.3 us
    dot_general x8, matrix products, contract(): lax.dot_general(left, right, (((0,), (0,)), ((), ())), preferred_element_...  38.5 us
    convert_element_type x2, local copies, waits for them, and re-layouts, local(): grad_qkv_w = jnp.stack([grad_query, grad_key, grad_value], axis=2).astype...  38.2 us
  transfers between devices with their start and end apart: 6, of which 4 were waited for; matrix products, arithmetic and copies ran while one was open for 14% of the time, Pallas kernels for 0%

commit v1 on v0

v1 whole, which is shorter than its diff:
```python
import functools
import math

import jax
import jax.numpy as jnp
from jax import lax
from jax.experimental import pallas as pl
from jax.experimental.pallas import tpu as pltpu
from jax.sharding import PartitionSpec as P

HEADS = 16
EPS = 1e-05
F32 = jnp.float32
BF16 = jnp.bfloat16
LOG2E = 1.4426950408889634
VMEM_LIMIT = 60 * 1024 * 1024
HIGH = lax.Precision.HIGHEST
LANES = 128
SEG = 64


def mm(a, b):
    return lax.dot_general(a, b, (((1,), (0,)), ((), ())), preferred_element_type=F32)


def mm_nt(a, b):
    return lax.dot_general(a, b, (((1,), (1,)), ((), ())), preferred_element_type=F32)


def mm_tn(a, b):
    return lax.dot_general(a, b, (((0,), (0,)), ((), ())), preferred_element_type=F32)


def norm_stats(v):
    average = jnp.mean(v, axis=-1, keepdims=True)
    centered = v - average
    variance = jnp.mean(centered * centered, axis=-1, keepdims=True)
    rstd = lax.rsqrt(variance + EPS)
    return centered * rstd, rstd


def norm_back(hat, rstd, gain, dn):
    dhat = dn * gain
    m1 = jnp.mean(dhat, axis=-1, keepdims=True)
    m2 = jnp.mean(dhat * hat, axis=-1, keepdims=True)
    return rstd * (dhat - m1 - hat * m2)


def colsum(v):
    return jnp.sum(v, axis=0, keepdims=True)


def gelu_both(u):
    a = jnp.abs(u)
    d = 1.0 + (0.3275911 * 0.7071067811865476) * a
    r = pl.reciprocal(d, approx=True)
    t = r * (2.0 - d * r)
    e = jnp.exp2((u * u) * (-0.5 * LOG2E))
    poly = t * (
        0.127414796
        + t * (-0.142248368 + t * (0.7107068705 + t * (-0.7265760135 + t * 0.5307027145)))
    )
    tail = poly * e
    cdf = jnp.where(u >= 0.0, 1.0 - tail, tail)
    return u * cdf, cdf + u * (e * 0.3989422804014327)


def head_masks(rows, head_dim):
    lane = lax.broadcasted_iota(jnp.int32, (rows, LANES), 1)
    return [(lane // head_dim) == h for h in range(LANES // head_dim)]


def spread(v, masks):
    zero = jnp.zeros_like(v)
    return jnp.concatenate([jnp.where(m, v, zero) for m in masks], axis=0)


def unspread(full, rows, stride, masks):
    out = full[(len(masks) - 1) * stride : (len(masks) - 1) * stride + rows]
    for h in range(len(masks) - 2, -1, -1):
        out = jnp.where(masks[h][:rows], full[h * stride : h * stride + rows], out)
    return out


def one_hot(code_col, count):
    rows = code_col.shape[0]
    return (lax.broadcasted_iota(jnp.int32, (rows, count), 1) == code_col).astype(F32).astype(BF16)


def one_hot_t(code_row, count):
    rows = code_row.shape[1]
    return (lax.broadcasted_iota(jnp.int32, (count, rows), 0) == code_row).astype(F32).astype(BF16)


def whole(*shape):
    return pl.BlockSpec(shape, lambda *_: (0,) * len(shape))


class Sizes:
    def __init__(self, per_dev, patch_tokens, width, count_gx):
        self.w = per_dev
        self.tok = patch_tokens
        self.d = width
        self.nb = count_gx
        self.k = per_dev // count_gx
        step = 16 // math.gcd(16, self.k)
        self.pos = -(-(patch_tokens + 1) // step) * step
        self.gp = step
        while (self.gp * self.k) % 16:
            self.gp *= 2
        self.ng = self.pos // self.gp
        self.r = self.pos * self.k
        self.wide = 56 * self.k
        self.hd = width // HEADS
        self.groups = width // LANES
        self.per_group = LANES // self.hd
        self.chunk = self.r // 3 if self.r % 48 == 0 else self.r


def params(**kw):
    return pltpu.CompilerParams(vmem_limit_bytes=VMEM_LIMIT, **kw)


def pack_kernel(z, x_ref, first_ref, code_ref, out_ref):
    sel = one_hot(code_ref[...], z.gp * z.w)
    for g in range(z.ng):
        pack_group(z, g, sel, x_ref, first_ref, out_ref)


def pack_group(z, g, sel, x_ref, first_ref, out_ref):
    pieces = []
    for p in range(g * z.gp, (g + 1) * z.gp):
        if p == 0:
            pieces.append(jnp.zeros((z.w, z.d), BF16) if first_ref is None else first_ref[...])
        elif p <= z.tok:
            pieces.append(x_ref[p - 1])
        else:
            pieces.append(jnp.zeros((z.w, z.d), BF16))
    got = mm(sel, jnp.concatenate(pieces, axis=0)).astype(BF16)
    rows = z.gp * z.k
    for c in range(z.nb):
        out_ref[c, g * rows : (g + 1) * rows, :] = got[c * rows : (c + 1) * rows]


def unpack_group(z, g, sel_t, packed_ref, out_ref, first_ref):
    rows = z.gp * z.k
    src = jnp.concatenate([packed_ref[c, g * rows : (g + 1) * rows, :] for c in range(z.nb)], axis=0)
    got = mm(sel_t, src).astype(BF16)
    for i in range(z.gp):
        p = g * z.gp + i
        piece = got[i * z.w : (i + 1) * z.w]
        if p == 0:
            if first_ref is not None:
                first_ref[...] = piece
        elif p <= z.tok:
            out_ref[p - 1] = piece


def unpack_kernel(z, *refs):
    packed, code_ref, out_ref, first_ref = refs[: z.nb], refs[z.nb], refs[z.nb + 1], refs[z.nb + 2]
    sel_t = one_hot_t(code_ref[...], z.gp * z.w)
    rows = z.gp * z.k
    for g in range(z.ng):
        src = jnp.concatenate([packed[c][g * rows : (g + 1) * rows, :] for c in range(z.nb)], axis=0)
        got = mm(sel_t, src).astype(BF16)
        for i in range(z.gp):
            p = g * z.gp + i
            piece = got[i * z.w : (i + 1) * z.w]
            if p == 0:
                first_ref[...] = piece
            elif p <= z.tok:
                out_ref[p - 1] = piece


def qkv_kernel(z, x_ref, code_ref, gain_ref, shift_ref, w_ref, xp_ref, qkv_ref):
    sel = one_hot(code_ref[...], z.gp * z.w)
    for g in range(z.ng):
        pack_group(z, g, sel, x_ref, None, xp_ref)
    per = z.r // z.chunk

    def body(i, _):
        c, rows = i // per, pl.ds(pl.multiple_of((i % per) * z.chunk, 16), z.chunk)
        hat, _ = norm_stats(xp_ref[c, rows, :].astype(F32))
        nt = (hat * gain_ref[...] + shift_ref[...]).astype(BF16)
        qkv_ref[c, rows, :] = mm(nt, w_ref[...]).astype(BF16)
        return 0

    lax.fori_loop(0, z.nb * per, body, 0)


def region_fwd_kernel(
    z, kc, all_ref, own_ref, imgk_ref, imgq_ref, ord_ref, gain_ref, shift_ref, w_ref, wo_ref, bo_ref,
    r2_ref, p_ref, kv_ref, nr_ref, q_ref, o_ref, of_ref, nown_ref, s_ref,
):
    n = all_ref.shape[0]
    nq = HEADS * z.w
    hat, _ = norm_stats(own_ref[...].astype(F32))
    nown = (hat * gain_ref[...] + shift_ref[...]).astype(BF16)
    nown_ref[...] = nown
    q = mm(nown, w_ref[:, : z.d]).astype(BF16)
    q_ref[...] = q
    lane = lax.broadcasted_iota(jnp.int32, (z.w, z.d), 1) // z.hd
    zero = jnp.zeros_like(q)
    qbd = jnp.concatenate([jnp.where(lane == h, q, zero) for h in range(HEADS)], axis=0)
    scale = z.hd ** (-0.5) * LOG2E

    def scores(i, top):
        rows = pl.ds(pl.multiple_of(i * kc, kc), kc)
        hat, _ = norm_stats(all_ref[rows, :].astype(F32))
        nr = (hat * gain_ref[...] + shift_ref[...]).astype(BF16)
        nr_ref[rows, :] = nr
        kv = mm(nr, w_ref[:, z.d :]).astype(BF16)
        kv_ref[rows, :] = kv
        s = mm_nt(kv[:, : z.d], qbd) * scale
        s = jnp.where(imgk_ref[rows, :] == imgq_ref[...], s, -1e30)
        s_ref[rows, :] = s
        return jnp.maximum(top, jnp.max(s, axis=0, keepdims=True))

    top = lax.fori_loop(0, n // kc, scores, jnp.full((1, nq), -1e30, F32))

    def weigh(i, total):
        rows = pl.ds(pl.multiple_of(i * kc, kc), kc)
        p = jnp.exp2(s_ref[rows, :] - top)
        s_ref[rows, :] = p
        return total + jnp.sum(p, axis=0, keepdims=True)

    total = lax.fori_loop(0, n // kc, weigh, jnp.zeros((1, nq), F32))
    inverse = 1.0 / total

    def attend(i, acc):
        rows = pl.ds(pl.multiple_of(i * kc, kc), kc)
        p = (s_ref[rows, :] * inverse).astype(BF16)
        p_ref[rows, :] = p
        return acc + mm_tn(p, kv_ref[rows, z.d :])

    full = lax.fori_loop(0, n // kc, attend, jnp.zeros((nq, z.d), F32))
    o = full[(HEADS - 1) * z.w :]
    for h in range(HEADS - 2, -1, -1):
        o = jnp.where(lane == h, full[h * z.w : (h + 1) * z.w], o)
    of_ref[...] = o
    o = o.astype(BF16)
    o_ref[...] = o
    r2 = own_ref[...].astype(F32) + mm(o, wo_ref[...]) + bo_ref[...]
    sel = one_hot(ord_ref[...], z.w).astype(F32)
    r2 = jnp.dot(sel, r2, precision=HIGH, preferred_element_type=F32)
    for c in range(z.nb):
        r2_ref[c] = r2[c * z.k : (c + 1) * z.k]


def local_fwd_kernel(
    z, qkv_ref, xp_ref, r2_ref, gain_ref, shift_ref, w_ref, wo_ref, bo_ref,
    t2_ref, p_ref, qw_ref, o_ref, qs, os,
):
    tiles = 3 * z.groups
    for j in range(tiles):
        qs[j, : z.r, :] = qkv_ref[0, :, j * LANES : (j + 1) * LANES].astype(F32)
        if z.wide > z.r:
            qs[j, z.r :, :] = jnp.zeros((z.wide - z.r, LANES), F32)
    hat, _ = norm_stats(r2_ref[0])
    nt = (hat * gain_ref[...] + shift_ref[...]).astype(BF16)
    reg = mm(nt, w_ref[...]).astype(BF16).astype(F32)
    for j in range(tiles):
        qs[j, : z.k, :] = reg[:, j * LANES : (j + 1) * LANES]
    masks = head_masks(SEG, z.hd)
    pad = jnp.zeros((SEG - 56, LANES), F32)
    valid = lax.broadcasted_iota(jnp.int32, (56, z.per_group * SEG), 0) < z.tok + 1
    scale = z.hd ** (-0.5) * LOG2E

    def window(w, _):
        def load(j):
            rows = qs[j, pl.ds(w, 56, stride=z.k), :]
            got = jnp.concatenate([rows, pad], axis=0).astype(BF16)
            qw_ref[w, j] = got
            return got

        for g in range(z.groups):
            q, k, v = load(g), load(z.groups + g), load(2 * z.groups + g)
            s = mm_nt(k, spread(q, masks))[:56]
            s = jnp.where(valid, s, -1e30)
            p = jnp.exp2((s - jnp.max(s, axis=0, keepdims=True)) * scale)
            p = p * (1.0 / jnp.sum(p, axis=0, keepdims=True))
            p = jnp.concatenate([p, jnp.zeros((SEG - 56, z.per_group * SEG), F32)], axis=0).astype(BF16)
            p_ref[w, g] = p
            full = mm_tn(p, v)
            os[g, pl.ds(w, 56, stride=z.k), :] = unspread(full, 56, SEG, masks)
        return 0

    lax.fori_loop(0, z.k, window, 0)
    for i in range(z.r // z.chunk):
        rows = slice(i * z.chunk, (i + 1) * z.chunk)
        o = jnp.concatenate([os[g, rows, :] for g in range(z.groups)], axis=1).astype(BF16)
        o_ref[0, rows, :] = o
        t2_ref[0, rows, :] = xp_ref[0, rows, :].astype(F32) + mm(o, wo_ref[...]) + bo_ref[...]
    t2_ref[0, : z.k, :] = t2_ref[0, : z.k, :] + r2_ref[0]


def mlp_kernel(
    z, parts, t2_ref, e_ref, gain_ref, shift_ref, wu_ref, bu_ref, wd_ref, bd_ref,
    y_ref, gt_ref, gwu_ref, gwd_ref, small_ref, gbu_ref,
    n2_ref, h_ref, act_ref, gp_ref, yacc, dn, awu, awd,
):
    step = pl.program_id(0)
    steps = pl.num_programs(0)
    fc = wu_ref.shape[1] // parts

    @pl.when(step == 0)
    def _():
        awu[...] = jnp.zeros_like(awu)
        awd[...] = jnp.zeros_like(awd)
        small_ref[...] = jnp.zeros_like(small_ref)
        gbu_ref[...] = jnp.zeros_like(gbu_ref)

    sub = 48
    for i in range(z.r // sub):
        rows = slice(i * sub, (i + 1) * sub)
        hat, _ = norm_stats(t2_ref[0, rows, :])
        n2_ref[rows, :] = (hat * gain_ref[...] + shift_ref[...]).astype(BF16)

    def part(f, _):
        cols = pl.ds(pl.multiple_of(f * fc, fc), fc)
        h_ref[...] = mm(n2_ref[...], wu_ref[:, cols])
        bias = bu_ref[:, cols]
        for i in range(z.r // 16):
            rows = slice(i * 16, (i + 1) * 16)
            act, gp = gelu_both(h_ref[rows, :] + bias)
            act_ref[rows, :] = act.astype(BF16)
            gp_ref[rows, :] = gp
        e = e_ref[0]
        yacc[...] = jnp.where(f == 0, 0.0, yacc[...]) + mm(act_ref[...], wd_ref[cols, :])
        awd[cols, :] += mm_tn(act_ref[...], e)
        h_ref[...] = mm_nt(e, wd_ref[cols, :])
        total = jnp.zeros((1, fc), F32)
        for i in range(z.r // 16):
            rows = slice(i * 16, (i + 1) * 16)
            dh = (h_ref[rows, :] * gp_ref[rows, :]).astype(BF16)
            act_ref[rows, :] = dh
            total = total + colsum(dh.astype(F32))
        gbu_ref[:, cols] += total
        awu[:, cols] += mm_tn(n2_ref[...], act_ref[...])
        dn[...] = jnp.where(f == 0, 0.0, dn[...]) + mm_nt(act_ref[...], wu_ref[:, cols])
        return 0

    lax.fori_loop(0, parts, part, 0)
    sums = [jnp.zeros((1, z.d), F32) for _ in range(4)]
    for i in range(z.r // sub):
        rows = slice(i * sub, (i + 1) * sub)
        t2 = t2_ref[0, rows, :]
        e = e_ref[0, rows, :].astype(F32)
        y_ref[0, rows, :] = (t2 + yacc[rows, :] + bd_ref[...]).astype(BF16)
        hat, rstd = norm_stats(t2)
        d = dn[rows, :]
        gt = (e + norm_back(hat, rstd, gain_ref[...], d)).astype(BF16)
        gt_ref[0, rows, :] = gt
        sums = [
            sums[0] + colsum(d * hat),
            sums[1] + colsum(d),
            sums[2] + colsum(e),
            sums[3] + colsum(gt.astype(F32)),
        ]
    for i in range(4):
        small_ref[i : i + 1, :] += sums[i]

    @pl.when(step == steps - 1)
    def _():
        gwu_ref[...] = awu[...].astype(BF16)
        gwd_ref[...] = awd[...].astype(BF16)


def local_bwd_kernel(
    z, gt_ref, xp_ref, r2_ref, o_ref, p_ref, qw_ref, code_ref, gain_ref, shift_ref, w_ref, wo_ref,
    pg_ref, dt0_ref, gwq_ref, gwo_ref, small_ref,
    ds_, dq_, dqkv, dtp, hat_s,
):
    step = pl.program_id(0)
    steps = pl.num_programs(0)

    @pl.when(step == 0)
    def _():
        gwq_ref[...] = jnp.zeros_like(gwq_ref)
        gwo_ref[...] = jnp.zeros_like(gwo_ref)
        small_ref[...] = jnp.zeros_like(small_ref)

    gt = gt_ref[0]
    dot = mm_nt(gt, wo_ref[...])
    for j in range(z.groups):
        ds_[j, : z.r, :] = dot[:, j * LANES : (j + 1) * LANES]
        if z.wide > z.r:
            ds_[j, z.r :, :] = jnp.zeros((z.wide - z.r, LANES), F32)
    gwo_ref[...] += mm_tn(o_ref[0], gt)
    masks = head_masks(SEG, z.hd)
    pad = jnp.zeros((SEG - 56, LANES), F32)
    scale = z.hd ** (-0.5)

    def window(w, _):
        for g in range(z.groups):
            q, k, v = qw_ref[w, g], qw_ref[w, z.groups + g], qw_ref[w, 2 * z.groups + g]
            do = jnp.concatenate([ds_[g, pl.ds(w, 56, stride=z.k), :], pad], axis=0).astype(BF16)
            p = p_ref[w, g]
            dobd = spread(do, masks)
            dp = mm_nt(v, dobd)
            pf = p.astype(F32)
            t = pf * dp
            ds = (t - pf * jnp.sum(t, axis=0, keepdims=True)).astype(BF16)
            dv = mm(p, dobd)
            dk = mm(ds, spread(q, masks)) * scale
            dq = unspread(mm_tn(ds, k), 56, SEG, masks) * scale
            dq_[g, pl.ds(w, 56, stride=z.k), :] = dq
            dq_[z.groups + g, pl.ds(w, 56, stride=z.k), :] = dk[:56]
            dq_[2 * z.groups + g, pl.ds(w, 56, stride=z.k), :] = dv[:56]
        return 0

    lax.fori_loop(0, z.k, window, 0)
    for j in range(3 * z.groups):
        dqkv[:, j * LANES : (j + 1) * LANES] = dq_[j, : z.r, :].astype(BF16)
    dn = mm_nt(dqkv[...], w_ref[...])
    ds_flat = hat_s
    t = xp_ref[0].astype(F32)
    t = jnp.concatenate([r2_ref[0], t[z.k :]], axis=0)
    hat, rstd = norm_stats(t)
    nt = (hat * gain_ref[...] + shift_ref[...]).astype(BF16)
    gwq_ref[...] += mm_tn(nt, dqkv[...])
    dt = gt.astype(F32) + norm_back(hat, rstd, gain_ref[...], dn)
    dt0_ref[0] = dt[: z.k]
    dtp[step] = dt.astype(BF16)
    small_ref[0:1, :] += colsum(dn * hat)
    small_ref[1:2, :] += colsum(dn)

    @pl.when(step == steps - 1)
    def _():
        sel_t = one_hot_t(code_ref[...], z.gp * z.w)
        for g in range(z.ng):
            unpack_group(z, g, sel_t, dtp, pg_ref, None)


def region_bwd_kernel(
    z, kc, dt0_ref, all_ref, o_ref, of_ref, p_ref, kv_ref, nr_ref, q_ref, nown_ref, own_ref, ord_ref, gain_ref,
    w_ref, wo_ref,
    dnr_ref, dt0a_ref, dnown_ref, gwq_ref, gwo_ref, small_ref,
):
    n = all_ref.shape[0]
    nq = HEADS * z.w
    dt0 = jnp.concatenate([dt0_ref[c] for c in range(z.nb)], axis=0)
    sel_t = one_hot_t(ord_ref[...], z.w).astype(F32)
    dt0 = jnp.dot(sel_t, dt0, precision=HIGH, preferred_element_type=F32)
    dt0a_ref[...] = dt0
    gr = dt0.astype(BF16)
    gwo_ref[...] = mm_tn(o_ref[...], gr)
    do = mm_nt(gr, wo_ref[...]).astype(BF16)
    lane = lax.broadcasted_iota(jnp.int32, (z.w, z.d), 1) // z.hd
    zero = jnp.zeros_like(do)
    dobd = jnp.concatenate([jnp.where(lane == h, do, zero) for h in range(HEADS)], axis=0)
    q = q_ref[...]
    qbd = jnp.concatenate([jnp.where(lane == h, q, zero) for h in range(HEADS)], axis=0)
    scale = z.hd ** (-0.5)

    prod = do.astype(F32) * of_ref[...]
    spread_prod = jnp.concatenate([jnp.where(lane == h, prod, 0.0) for h in range(HEADS)], axis=0)
    delta = lax.dot_general(
        jnp.ones((8, z.d), F32), spread_prod, (((1,), (1,)), ((), ())), precision=HIGH,
        preferred_element_type=F32,
    )[0:1]
    small_ref[...] = jnp.zeros_like(small_ref)
    gwq_ref[...] = jnp.zeros_like(gwq_ref)

    def second(i, acc):
        rows = pl.ds(pl.multiple_of(i * kc, kc), kc)
        p = p_ref[rows, :]
        ds = (p.astype(F32) * (mm_nt(kv_ref[rows, z.d :], dobd) - delta)).astype(BF16)
        dv = mm(p, dobd).astype(BF16)
        dk = (mm(ds, qbd) * scale).astype(BF16)
        dkv = jnp.concatenate([dk, dv], axis=1)
        gwq_ref[:, z.d :] += mm_tn(nr_ref[rows, :], dkv)
        dn = mm_nt(dkv, w_ref[:, z.d :])
        dnr_ref[rows, :] = dn.astype(BF16)
        hat, _ = norm_stats(all_ref[rows, :].astype(F32))
        small_ref[0:1, :] += colsum(dn * hat)
        small_ref[1:2, :] += colsum(dn)
        return acc + mm_tn(ds, kv_ref[rows, : z.d])

    full = lax.fori_loop(0, n // kc, second, jnp.zeros((nq, z.d), F32))
    dq = full[(HEADS - 1) * z.w :]
    for h in range(HEADS - 2, -1, -1):
        dq = jnp.where(lane == h, full[h * z.w : (h + 1) * z.w], dq)
    dq = (dq * scale).astype(BF16)
    gwq_ref[:, : z.d] = mm_tn(nown_ref[...], dq)
    dn = mm_nt(dq, w_ref[:, : z.d])
    dnown_ref[...] = dn
    hat, _ = norm_stats(own_ref[...].astype(F32))
    small_ref[0:1, :] += colsum(dn * hat)
    small_ref[1:2, :] += colsum(dn)
    small_ref[2:3, :] = colsum(gr.astype(F32))


def local(
    patches, regions, send_order, image_windows, attn_gain, attn_shift, w_qkv, w_out, b_out,
    mlp_gain, mlp_shift, w_up, b_up, w_down, b_down, upstream_patches, upstream_regions,
):
    axes = ("gx", "gy")
    nx, ny = lax.axis_size("gx"), lax.axis_size("gy")
    z = Sizes(patches.shape[0], patches.shape[1], patches.shape[2], nx)
    ff = w_up.shape[1]
    n = z.w * nx * ny
    gx = lax.axis_index("gx")
    dev = gx * ny + lax.axis_index("gy")
    sds = jax.ShapeDtypeStruct

    order = lax.dynamic_slice_in_dim(send_order, dev, 1, 0)[0].reshape(nx, z.k)
    tile = jnp.arange(nx, dtype=jnp.int32)
    order_t = jnp.take(order, (gx - tile) % nx, axis=0)
    place = jnp.arange(z.gp, dtype=jnp.int32) * z.w
    code_x = (order_t[:, None, :] + place[None, :, None]).reshape(-1)
    block = ((gx + tile) % nx)[:, None] * z.k + jnp.arange(z.k, dtype=jnp.int32)[None, :]
    code_e = (block[:, None, :] + place[None, :, None]).reshape(-1)
    order_t = order_t.reshape(-1)
    bounds = jnp.cumsum(image_windows)
    image = jnp.sum(
        (jnp.arange(n, dtype=jnp.int32)[:, None] >= bounds[None, :]).astype(jnp.int32), axis=1
    )
    image_own = lax.dynamic_slice_in_dim(image, dev * z.w, z.w)
    gain, shift = attn_gain[None], attn_shift[None]

    x_t = jnp.transpose(patches, (1, 0, 2))
    e_t = jnp.transpose(upstream_patches, (1, 0, 2))

    packed = pl.pallas_call(
        functools.partial(pack_kernel, z),
        out_shape=sds((z.nb, z.r, z.d), BF16),
        compiler_params=params(),
        name="pack",
    )(e_t, upstream_regions, code_e[:, None])

    def exchange(blocks, sign):
        out = [blocks[0]]
        for o in range(1, nx):
            out.append(
                lax.ppermute(blocks[o], "gx", [(i, (i + sign * o) % nx) for i in range(nx)])
            )
        return out

    e_in = jnp.stack(exchange([packed[o] for o in range(nx)], 1))

    regions_all = lax.all_gather(regions, axes, axis=0, tiled=True)

    xp, qkv = pl.pallas_call(
        functools.partial(qkv_kernel, z),
        out_shape=(sds((z.nb, z.r, z.d), BF16), sds((z.nb, z.r, 3 * z.d), BF16)),
        compiler_params=params(),
        name="qkv",
    )(x_t, code_x[:, None], gain, shift, w_qkv)

    kc = 256
    nq = HEADS * z.w
    r2, p_r, kv_all, nr_all, q_r, o_r, o_f, n_own = pl.pallas_call(
        functools.partial(region_fwd_kernel, z, kc),
        out_shape=(
            sds((z.nb, z.k, z.d), F32),
            sds((n, nq), BF16),
            sds((n, 2 * z.d), BF16),
            sds((n, z.d), BF16),
            sds((z.w, z.d), BF16),
            sds((z.w, z.d), BF16),
            sds((z.w, z.d), F32),
            sds((z.w, z.d), BF16),
        ),
        scratch_shapes=[pltpu.VMEM((n, nq), F32)],
        compiler_params=params(),
        name="region_fwd",
    )(
        regions_all, regions, image[:, None], jnp.tile(image_own, HEADS)[None], order_t[:, None],
        gain, shift, w_qkv, w_out, b_out[None],
    )

    def tiled(*shape):
        return pl.BlockSpec((1,) + shape, lambda i: (i,) + (0,) * len(shape))

    def grouped(*shape):
        return pl.BlockSpec((z.k,) + shape, lambda i: (i,) + (0,) * len(shape))

    cols = z.per_group * SEG
    t2, p_w, qw, o_w = pl.pallas_call(
        functools.partial(local_fwd_kernel, z),
        grid=(z.nb,),
        in_specs=[
            tiled(z.r, 3 * z.d), tiled(z.r, z.d), tiled(z.k, z.d), whole(1, z.d), whole(1, z.d),
            whole(z.d, 3 * z.d), whole(z.d, z.d), whole(1, z.d),
        ],
        out_specs=[
            tiled(z.r, z.d), grouped(z.groups, SEG, cols), grouped(3 * z.groups, SEG, LANES),
            tiled(z.r, z.d),
        ],
        out_shape=(
            sds((z.nb, z.r, z.d), F32),
            sds((z.w, z.groups, SEG, cols), BF16),
            sds((z.w, 3 * z.groups, SEG, LANES), BF16),
            sds((z.nb, z.r, z.d), BF16),
        ),
        scratch_shapes=[
            pltpu.VMEM((3 * z.groups, z.wide, LANES), F32),
            pltpu.VMEM((z.groups, z.wide, LANES), F32),
        ],
        compiler_params=params(),
        name="local_fwd",
    )(qkv, xp, r2, gain, shift, w_qkv, w_out, b_out[None])

    parts = 4
    fc = ff // parts
    y, gt, gwu, gwd, small_m, gbu = pl.pallas_call(
        functools.partial(mlp_kernel, z, parts),
        grid=(z.nb,),
        in_specs=[
            tiled(z.r, z.d), tiled(z.r, z.d), whole(1, z.d), whole(1, z.d), whole(z.d, ff),
            whole(1, ff), whole(ff, z.d), whole(1, z.d),
        ],
        out_specs=[
            tiled(z.r, z.d), tiled(z.r, z.d), whole(z.d, ff), whole(ff, z.d), whole(8, z.d),
            whole(1, ff),
        ],
        out_shape=(
            sds((z.nb, z.r, z.d), BF16),
            sds((z.nb, z.r, z.d), BF16),
            sds((z.d, ff), BF16),
            sds((ff, z.d), BF16),
            sds((8, z.d), F32),
            sds((1, ff), F32),
        ),
        scratch_shapes=[
            pltpu.VMEM((z.r, z.d), BF16),
            pltpu.VMEM((z.r, fc), F32),
            pltpu.VMEM((z.r, fc), BF16),
            pltpu.VMEM((z.r, fc), F32),
            pltpu.VMEM((z.r, z.d), F32),
            pltpu.VMEM((z.r, z.d), F32),
            pltpu.VMEM((z.d, ff), F32),
            pltpu.VMEM((ff, z.d), F32),
        ],
        compiler_params=params(),
        name="mlp",
    )(t2, e_in, mlp_gain[None], mlp_shift[None], w_up, b_up[None], w_down, b_down[None])

    y_in = exchange([y[o] for o in range(nx)], -1)
    out_p, out_r = pl.pallas_call(
        functools.partial(unpack_kernel, z),
        out_shape=(sds((z.tok, z.w, z.d), BF16), sds((z.w, z.d), BF16)),
        compiler_params=params(),
        name="unpack",
    )(*y_in, code_e[None])

    patch_grad, dt0, gwq, gwo, small_a = pl.pallas_call(
        functools.partial(local_bwd_kernel, z),
        grid=(z.nb,),
        in_specs=[
            tiled(z.r, z.d), tiled(z.r, z.d), tiled(z.k, z.d), tiled(z.r, z.d),
            grouped(z.groups, SEG, cols), grouped(3 * z.groups, SEG, LANES),
            whole(1, z.nb * z.gp * z.k), whole(1, z.d), whole(1, z.d), whole(z.d, 3 * z.d),
            whole(z.d, z.d),
        ],
        out_specs=[
            whole(z.tok, z.w, z.d), tiled(z.k, z.d), whole(z.d, 3 * z.d), whole(z.d, z.d),
            whole(8, z.d),
        ],
        out_shape=(
            sds((z.tok, z.w, z.d), BF16),
            sds((z.nb, z.k, z.d), F32),
            sds((z.d, 3 * z.d), F32),
            sds((z.d, z.d), F32),
            sds((8, z.d), F32),
        ),
        scratch_shapes=[
            pltpu.VMEM((z.groups, z.wide, LANES), F32),
            pltpu.VMEM((3 * z.groups, z.wide, LANES), F32),
            pltpu.VMEM((z.r, 3 * z.d), BF16),
            pltpu.VMEM((z.nb, z.r, z.d), BF16),
            pltpu.VMEM((8, LANES), F32),
        ],
        compiler_params=params(),
        name="local_bwd",
    )(gt, xp, r2, o_w, p_w, qw, code_x[None], gain, shift, w_qkv, w_out)

    dnr, dt0a, dn_own, gwq_r, gwo_r, small_r = pl.pallas_call(
        functools.partial(region_bwd_kernel, z, kc),
        out_shape=(
            sds((n, z.d), BF16),
            sds((z.w, z.d), F32),
            sds((z.w, z.d), F32),
            sds((z.d, 3 * z.d), F32),
            sds((z.d, z.d), F32),
            sds((8, z.d), F32),
        ),
        compiler_params=params(),
        name="region_bwd",
    )(
        dt0, regions_all, o_r, o_f, p_r, kv_all, nr_all, q_r, n_own, regions, order_t[None], gain, w_qkv,
        w_out,
    )

    dnr_own = lax.psum_scatter(dnr, axes, scatter_dimension=0, tiled=True).astype(F32) + dn_own
    hat, rstd = norm_stats(regions.astype(F32))
    region_grad = (dt0a + norm_back(hat, rstd, gain, dnr_own)).astype(BF16)

    gwq = (gwq + gwq_r).astype(BF16)
    gwo = (gwo + gwo_r).astype(BF16)
    small_a = small_a + small_r
    gwu, gwd, gwq, gwo = lax.psum((gwu, gwd, gwq, gwo), axes)
    g_again, g_ashift, g_bout, g_mgain, g_mshift, g_bdown, g_bup = lax.psum(
        (small_a[0], small_a[1], small_a[2] + small_m[3], small_m[0], small_m[1], small_m[2], gbu[0]),
        axes,
    )
    return (
        jnp.transpose(out_p, (1, 0, 2)),
        out_r,
        jnp.transpose(patch_grad, (1, 0, 2)),
        region_grad,
        g_again,
        g_ashift,
        gwq.astype(F32),
        gwo.astype(F32),
        g_bout,
        g_mgain,
        g_mshift,
        gwu.astype(F32),
        g_bup,
        gwd.astype(F32),
        g_bdown,
    )


def solution(mesh):
    split = ("gx", "gy")
    rows3, rows2, full = P(split, None, None), P(split, None), P()
    in_specs = (rows3, rows2) + (full,) * 13 + (rows3, rows2)
    out_specs = (rows3, rows2, rows3, rows2) + (full,) * 11
    return jax.shard_map(local, mesh=mesh, in_specs=in_specs, out_specs=out_specs, check_vma=False)
```

time: 983 us -> 560 us (0.57); the launches traced: 969 us -> 560 us
  local copies, waits for them, and re-layouts: 296 us -> 13.7 us
  matrix products: 267 us -> 0 us
  Pallas kernels: 0 us -> 238 us
  other arithmetic: 96.4 us -> 21.9 us
  waiting for transfers between devices: 229 us -> 205 us
    dot_general x31 -> x0, matrix products: 264 us -> none  [the longest x6 78.9 us: matmul(): return jnp.dot(left, right, preferred_element_type=jnp.float32)]
    pallas_call x0 -> x8, Pallas kernels: none -> 238 us  [the longest x1 68.8 us: local(): pl.pallas_call(functools.partial(local_bwd_kernel, z), grid=(z.nb,), in_s...]
    reshape x10 -> x0, local copies, waits for them, and re-layouts: 79.6 us -> none  [the longest x1 32.3 us: local(): qkv_w = matmul(normed_w, w_qkv).astype(jnp.bfloat16).reshape(per_dev, seq...]
    unnamed x181 -> x38, local copies, waits for them, and re-layouts: 71.8 us -> 2.96 us
    convert_element_type x6 -> x0, local copies, waits for them, and re-layouts: 61.3 us -> none  [the longest x2 38.2 us: local(): grad_qkv_w = jnp.stack([grad_query, grad_key, grad_value], axis=2).astype...]
    reduce_scatter x1, waiting for transfers between devices: 70.3 us -> 17.9 us  [local(): lax.psum_scatter(dnr, axes, scatter_dimension=0, tiled=True).astype(F32)]
    psum x1, waiting for transfers between devices: 119 us -> 160 us  [local(): gwu, gwd, gwq, gwo = lax.psum((gwu, gwd, gwq, gwo), axes)]
    all_to_all x3 -> x0, waiting for transfers between devices: 40.3 us -> none  [the longest x1 29.5 us: local(): lax.all_to_all(patch_dealt, 'gx', split_axis=0, concat_axis=0, tiled=True)]
  transfers between devices with their start and end apart: 6 -> 9, of which waited for: 4 -> 4; matrix products, arithmetic and copies ran while one was open for 14% -> 4% of each run, Pallas kernels for 0% -> 4%
where the time goes in v1:
time: 560 us
  Pallas kernels  238 us (42%)
  waiting for transfers between devices  205 us (37%)
  blocking collectives  60.3 us (11%)
  other arithmetic  21.9 us (4%)
  between operations  14 us (2%)
  local copies, waits for them, and re-layouts  13.7 us (2%)
  starting transfers between devices  6.23 us (1%)
    psum x1, waiting for transfers between devices, local(): gwu, gwd, gwq, gwo = lax.psum((gwu, gwd, gwq, gwo), axes)  160 us
    pallas_call x1, Pallas kernels, local(): pl.pallas_call(functools.partial(local_bwd_kernel, z), grid=(z.nb,), in_s...  68.8 us
    pallas_call x1, Pallas kernels, local(): pl.pallas_call(functools.partial(mlp_kernel, z, parts), grid=(z.nb,), in_...  68.4 us
    psum x1, blocking collectives, local(): lax.psum((small_a[0], small_a[1], small_a[2] + small_m[3], small_m[0], sm...  60.3 us
    pallas_call x1, Pallas kernels, local(): pl.pallas_call(functools.partial(local_fwd_kernel, z), grid=(z.nb,), in_s...  44.9 us
    pallas_call x1, Pallas kernels, local(): pl.pallas_call(functools.partial(region_bwd_kernel, z, kc), out_shape=(sd...  19.4 us
    reduce_scatter x1, waiting for transfers between devices, local(): lax.psum_scatter(dnr, axes, scatter_dimension=0, tiled=True).astype(F32)  17.9 us
    all_gather x1, waiting for transfers between devices, local(): regions_all = lax.all_gather(regions, axes, axis=0, tiled=True)  17 us
  transfers between devices with their start and end apart: 9, of which 4 were waited for; matrix products, arithmetic and copies ran while one was open for 4% of the time, Pallas kernels for 4%

profile of v1, /device:TPU:0, one launch (start us, length us, event | category | flops | bytes accessed | tf_op | source)
XLA Modules:
  0.0 559.6 jit_solution(7876399417994605279)
XLA Ops:
  7.2 0.0 copy-start
  7.2 0.0 all-gather.2.cloned.1.call-start
  7.2 0.7 all-gather.2.cloned.1.call-update
  7.9 0.0 reduce-scatter.2.cloned.1.call-start
  8.0 0.1 reshape_squeeze.3
  8.1 0.6 gather_fusion
  8.7 0.1 iota_add_fusion
  8.8 0.1 broadcast_select_fusion
  8.9 0.1 broadcast_add_fusion
  9.0 0.7 add.227.code_ref
  9.7 4.1 pack.1
  13.7 2.7 fusion.16
  16.5 2.4 collective-permute-start.2
  18.9 0.6 collective-permute-start.1
  19.5 0.2 collective-permute-start
  19.7 0.6 select_n.85.ord_ref
  20.3 0.7 select_n.86.ord_ref
  21.0 0.7 add.216.code_ref
  21.6 0.7 add.226.code_ref
  22.4 0.1 copy.40
  22.5 0.1 reduce-window.8
  22.5 0.1 reduce.1
  22.6 0.1 convert_reduce_fusion
  22.8 1.1 broadcast_in_dim.57.imgk_ref
  23.9 0.1 dynamic_slice.7
  24.0 0.7 broadcast_in_dim_tile.3.imgq_ref
  24.7 14.7 %qkv.1 = (bf16[4,624,512]{2,1,0:T(8,128)(2,1)}, bf16[4,624,1536]{2,1,0:T(8,128)(2,1)}) custom-call(bf16[49,48,512]{2,1,0:T(8,128)(2,1)} %bitcast.39, s32[192,1]{1,0:T(8,128)} %add.226.code_ref, f32[1,512]{1,0:T(1,128)} %bitcast.42, f32[1,512]{1,0:T(1,128)} %bitcast.47, bf16[512,1536]{1,0:T(8,128)(2,1)} %w_ref.9), custom_call_target="tpu_custom_call" | custom-call | tf_op jit(solution)/shard_map/qkv/pallas_call | solution.py:544
  39.4 9.9 %collective-permute-done.1 = bf16[624,512]{1,0:T(8,128)(2,1)S(1)} collective-permute-done((bf16[624,512]{1,0:T(8,128)(2,1)S(1)}, bf16[624,512]{1,0:T(8,128)(2,1)S(1)}, u32[]{:S(2)}, u32[]{:S(2)}) %collective-permute-start.1) | collective-permute-done | bytes 639008 | tf_op jit(solution)/shard_map/ppermute | solution.py:536
  49.3 2.9 pad_maximum_fusion.e_ref
  52.1 17.0 %all-gather.2.cloned.1.call-done.all_ref = bf16[1536,512]{1,0:T(8,128)(2,1)} async-done(((bf16[48,512]{1,0:T(8,128)(2,1)}), bf16[1536,512]{1,0:T(8,128)(2,1)}) %all-gather.2.cloned.1.call-update) | async-done | bytes 1572880 | tf_op jit(solution)/shard_map/all_gather | solution.py:542
  69.2 14.1 %region_fwd.1 = (f32[4,12,512]{2,1,0:T(8,128)}, bf16[1536,768]{1,0:T(8,128)(2,1)}, bf16[1536,1024]{1,0:T(8,128)(2,1)}, bf16[1536,512]{1,0:T(8,128)(2,1)}, bf16[4...) custom-call(bf16[1536,512]{1,0:T(8,128)(2,1)} %all-gather.2.cloned.1.call-done.all_ref, ...), custom_call_target="tpu_custom_call" | custom-call | tf_op jit(solution)/shard_map/region_fwd/pallas_call | solution.py:553
  83.3 44.9 %local_fwd.1 = (f32[4,624,512]{2,1,0:T(8,128)}, bf16[48,4,64,256]{3,2,1,0:T(8,128)(2,1)}, bf16[48,12,64,128]{3,2,1,0:T(8,128)(2,1)}, bf16[4,624,512]{2,1,0:T(8,128)(2,1)}) custom-call(bf16[4,624,1536]{2,1,0:T(8,128)(2,1)} %get-tuple-element.48.qkv_ref, bf16[4,624,512]{2,1,0:T(8,128)(2,1)} %get-tuple-element.49.xp_ref, ...), custom_call_target="tpu_custom_call" | custom-call | tf_op jit(solution)/shard_map/local_fwd/pallas_call | solution.py:580
  128.1 68.4 %mlp.1 = (bf16[4,624,512]{2,1,0:T(8,128)(2,1)}, bf16[4,624,512]{2,1,0:T(8,128)(2,1)}, bf16[512,2048]{1,0:T(8,128)(2,1)}, bf16[2048,512]{1,0:T(8,128)(2,1)}, f32[8,512]{1,0:T(8,128)}, /*index=5*/f32[1,2048]{1,0:T(1,128)}) custom-call(f32[4,624,512]{2,1,0:T(8,128)} %get-tuple-element.51.t2_ref, bf16[4,624,512]{2,1,0:T(8,128)(2,1)} %pad_maximum_fusion.e_ref, ...), custom_call_target="tpu_custom_call" | custom-call | tf_op jit(solution)/shard_map/mlp/pallas_call | solution.py:607
  196.5 68.8 %local_bwd.1 = (bf16[49,48,512]{2,1,0:T(8,128)(2,1)}, f32[4,12,512]{2,1,0:T(8,128)}, f32[512,1536]{1,0:T(8,128)}, f32[512,512]{1,0:T(8,128)}, f32[8,512]{1,0:T(8,128)}) custom-call(bf16[4,624,512]{2,1,0:T(8,128)(2,1)} %get-tuple-element.55.gt_ref, bf16[4,624,512]{2,1,0:T(8,128)(2,1)} %get-tuple-element.49.xp_ref, f32[4,12,512]{2,1,0:T(8,128)} %get-tuple-element.50.r2_ref, ...), custom_call_target="tpu_custom_call" | custom-call | tf_op jit(solution)/shard_map/local_bwd/pallas_call | solution.py:648
  265.3 19.4 %region_bwd.1 = (bf16[1536,512]{1,0:T(8,128)(2,1)}, f32[48,512]{1,0:T(8,128)}, f32[48,512]{1,0:T(8,128)}, f32[512,1536]{1,0:T(8,128)}, f32[512,512]{1,0:T(8,128)}, /*index=5*/f32[8,512]{1,0:T(8,128)}) custom-call(f32[4,12,512]{2,1,0:T(8,128)} %get-tuple-element.60.dt0_ref, bf16[1536,512]{1,0:T(8,128)(2,1)} %all-gather.2.cloned.1.call-done.all_ref, ...), custom_call_target="tpu_custom_call" | custom-call | tf_op jit(solution)/shard_map/region_bwd/pallas_call | solution.py:679
  284.7 0.0 reduce-scatter.2.cloned.1.call-update
  284.8 0.0 all-reduce.4.cloned.1.call-start
  284.8 2.7 add_convert_fusion.1
  287.5 3.5 add_convert_fusion
  291.0 0.0 all-reduce.4.cloned.1.call-update
  291.0 0.8 copy-done.4
  291.8 0.1 convert_reduce_fusion.1
  291.9 0.9 copy-done.3
  292.7 1.3 slice_bitcast_fusion.3
  294.0 0.3 collective-permute-start.5
  294.3 1.5 collective-permute-start.4
  295.8 1.2 collective-permute-start.3
  297.0 0.7 add.215.refs_4_
  297.6 0.2 fusion.9
  297.9 60.3 %all-reduce = (f32[512]{0:T(512)}, f32[512]{0:T(512)}, f32[512]{0:T(512)}, f32[512]{0:T(512)}, f32[512]{0:T(512)}, /*index=5*/f32[2048]{0:T(1024)}, f32[512]{0:T(512)}) all-reduce(f32[512]{0:T(512)S(1)} %bitcast.59, f32[512]{0:T(512)S(1)} %bitcast.58, f32[512]{0:T(512)S(1)} %bitcast.57, ...), channel_id=1, replica_groups=mesh['gx'=4,'gy'=8] {'gx','gy'}, use_global_device_ids=true, to_apply=%region_7.8 | all-reduce | flops 5120 | bytes 40960 | tf_op jit(solution)/shard_map/psum | solution.py:704
  358.2 0.0 copy-start.10
  358.2 0.8 copy-done.8
  359.0 0.2 copy-done.9
  359.2 0.2 copy-done.10
  359.4 3.9 unpack.1
  363.3 17.9 %reduce-scatter.2.cloned.1.call-done = bf16[48,512]{1,0:T(8,128)(2,1)} async-done(((bf16[1536,512]{1,0:T(8,128)(2,1)}), bf16[48,512]{1,0:T(8,128)(2,1)}) %reduce-scatter.2.cloned.1.call-update) | async-done | bytes 49168 | tf_op jit(solution)/shard_map/reduce_scatter | solution.py:696
  381.2 1.0 fusion.10
  382.2 1.5 fusion.8
  383.7 159.8 %all-reduce.4.cloned.1.call-done = (bf16[512,1536]{1,0:T(8,128)(2,1)}, bf16[512,512]{1,0:T(8,128)(2,1)}, bf16[512,2048]{1,0:T(8,128)(2,1)}, bf16[2048,512]{1,0:T(8,128)(2,1)}) async-done(((bf16[512,1536]{1,0:T(8,128)(2,1)}, bf16[512,512]{1,0:T(8,128)(2,1)}, bf16[512,2048]{1,0:T(8,128)(2,1)}, bf16[2048,512]{1,0:T(8,128)(2,1)}), (bf16[512,1536]{1,0:T(8,128)(2,1)}, bf16[512,512]{1,0:T(8,128)(2,1)}, ...) | async-done | bytes 6291472 | tf_op jit(solution)/shard_map/psum | solution.py:703
  543.6 2.3 convert_element_type.37
  545.8 2.1 convert_element_type.35
  547.9 0.0 copy-done.6
  548.0 2.5 convert_element_type.38
  550.5 2.6 convert_element_type.39
  (47 shorter events, 0.2 us)
Async XLA Ops:
  7.2 0.8 copy-start
  7.2 62.0 %all-gather.2.cloned.1.call-start = ((), (), s32[]{:S(2)}) async-start(), calls=%async_computation.1 | async-start | bytes 1622016 | tf_op jit(solution)/shard_map/all_gather | solution.py:542
  7.9 373.3 %reduce-scatter.2.cloned.1.call-start = ((), (), s32[]{:S(2)}) async-start(), calls=%async_computation.2 | async-start | bytes 1622016 | tf_op jit(solution)/shard_map/reduce_scatter | solution.py:696
  13.7 8.6 %copy-start.18 = (s32[48]{0:T(128)S(1)}, s32[48]{0:T(128)}, u32[]{:S(2)}) copy-start(s32[48]{0:T(128)} %param.20) | copy-start | bytes 580
  16.5 22.9 %collective-permute-start.2 = (bf16[624,512]{1,0:T(8,128)(2,1)}, bf16[624,512]{1,0:T(8,128)(2,1)S(1)}, u32[]{:S(2)}, u32[]{:S(2)}) collective-permute-start(bf16[624,512]{1,0:T(8,128)(2,1)} %get-tuple-element.99), channel_id=1, source_target_pairs={{0,24},{8,0},{16,8},{24,16},{1,25},{9,1},{17,9},{25,17},{2,26},{10... | collective-permute-start | bytes 1916936 | tf_op jit(solution)/shard_map/ppermute | solution.py:536
  18.9 30.4 %collective-permute-start.1 = (bf16[624,512]{1,0:T(8,128)(2,1)S(1)}, bf16[624,512]{1,0:T(8,128)(2,1)S(1)}, u32[]{:S(2)}, u32[]{:S(2)}) collective-permute-start(bf16[624,512]{1,0:T(8,128)(2,1)S(1)} %get-tuple-element.100), channel_id=1, source_target_pairs={{0,16},{8,24},{16,0},{24,8},{1,17},{9,25},{17,1},{25,9},{2,18},{10... | collective-permute-start | bytes 1916936 | tf_op jit(solution)/shard_map/ppermute | solution.py:536
  19.5 29.8 %collective-permute-start = (bf16[624,512]{1,0:T(8,128)(2,1)S(1)}, bf16[624,512]{1,0:T(8,128)(2,1)}, u32[]{:S(2)}, u32[]{:S(2)}) collective-permute-start(bf16[624,512]{1,0:T(8,128)(2,1)S(1)} %get-tuple-element.101), channel_id=1, source_target_pairs={{0,8},{8,16},{16,24},{24,0},{1,9},{9,17},{17,25},{25,1},{2,10},{10... | collective-permute-start | bytes 1916936 | tf_op jit(solution)/shard_map/ppermute | solution.py:536
  284.7 2.7 copy-start.2
  284.8 258.8 %all-reduce.4.cloned.1.call-start = ((), (), s32[]{:S(2)}) async-start(), calls=%async_computation.3 | async-start | bytes 12582912 | tf_op jit(solution)/shard_map/psum | solution.py:703
  291.0 0.8 copy-start.4
  291.0 1.8 copy-start.3
  292.7 5.1 copy-start.14
  292.7 5.1 copy-start.15
  292.7 5.1 copy-start.17
  292.7 5.1 copy-start.16
  294.0 87.2 %copy-start.11 = (f32[48,512]{1,0:T(8,128)S(1)}, f32[48,512]{1,0:T(8,128)}, u32[]{:S(2)}) copy-start(f32[48,512]{1,0:T(8,128)} %get-tuple-element.70) | copy-start | bytes 294916
  294.0 87.2 %copy-start.12 = (f32[512]{0:T(512)S(1)}, f32[512]{0:T(512)}, u32[]{:S(2)}) copy-start(f32[512]{0:T(512)} %param.21) | copy-start | bytes 6148
  294.0 88.2 %copy-start.13 = (f32[48,512]{1,0:T(8,128)S(1)}, f32[48,512]{1,0:T(8,128)}, u32[]{:S(2)}) copy-start(f32[48,512]{1,0:T(8,128)} %get-tuple-element.68) | copy-start | bytes 294916
  294.0 64.1 %collective-permute-start.5 = (bf16[624,512]{1,0:T(8,128)(2,1)}, bf16[624,512]{1,0:T(8,128)(2,1)S(1)}, u32[]{:S(2)}, u32[]{:S(2)}) collective-permute-start(bf16[624,512]{1,0:T(8,128)(2,1)} %get-tuple-element.94), channel_id=1, source_target_pairs={{0,8},{8,16},{16,24},{24,0},{1,9},{9,17},{17,25},{25,1},{2,10},{10... | collective-permute-start | bytes 1916936 | tf_op jit(solution)/shard_map/ppermute | solution.py:536
  294.3 63.9 %collective-permute-start.4 = (bf16[624,512]{1,0:T(8,128)(2,1)}, bf16[624,512]{1,0:T(8,128)(2,1)S(1)}, u32[]{:S(2)}, u32[]{:S(2)}) collective-permute-start(bf16[624,512]{1,0:T(8,128)(2,1)} %get-tuple-element.95), channel_id=1, source_target_pairs={{0,16},{8,24},{16,0},{24,8},{1,17},{9,25},{17,1},{25,9},{2,18},{10... | collective-permute-start | bytes 1916936 | tf_op jit(solution)/shard_map/ppermute | solution.py:536
  295.8 62.4 %collective-permute-start.3 = (bf16[624,512]{1,0:T(8,128)(2,1)S(1)}, bf16[624,512]{1,0:T(8,128)(2,1)S(1)}, u32[]{:S(2)}, u32[]{:S(2)}) collective-permute-start(bf16[624,512]{1,0:T(8,128)(2,1)S(1)} %get-tuple-element.96), channel_id=1, source_target_pairs={{0,24},{8,0},{16,8},{24,16},{1,25},{9,1},{17,9},{25,17},{2,26},{10... | collective-permute-start | bytes 1916936 | tf_op jit(solution)/shard_map/ppermute | solution.py:536
  358.2 0.9 copy-start.8
  358.2 1.0 copy-start.9
  358.2 1.2 copy-start.10
  543.6 2.3 copy-start.7
  545.8 2.1 copy-start.6
  547.9 2.5 copy-start.5
  550.5 2.6 copy-start.1
Sparse Core Ops, SparseCore 0:
  11.0 58.1 all-gather.1
  284.9 96.2 reduce-scatter.1
  387.8 155.6 all-reduce.3
